TPU v7x, 128 devices: a whole 4x4x4 slice. The times are simulated.
128 devices in a mesh: lat: 4 (over x_hi, core), lon: 32 (over y, x_lo, z).
Axes of the slice: x: 4 (x_hi: 2, x_lo: 2; x = x_hi * 2 + x_lo), y: 4, z: 4, core: 2. Of those that a mesh axis runs over, the one named last changes fastest.
Arguments:
- encoded: bfloat16 [2, 24, 512, 384], P(None, 'lat', 'lon'), may hold values from -6 to 6
- upstream: bfloat16 [2, 24, 384, 512], P(None, 'lat', 'lon'), may hold values from -6 to 6
- w_qkv: bfloat16 [2, 512, 1536], replicated, may hold values from -0.25 to 0.25
- w_proj: bfloat16 [2, 512, 512], replicated, may hold values from -0.25 to 0.25
- w_up: bfloat16 [2, 512, 2048], replicated, may hold values from -0.25 to 0.25
- w_down: bfloat16 [2, 2048, 512], replicated, may hold values from -0.125 to 0.125
Outputs:
- mixed: bfloat16 [2, 24, 384, 512], P(None, 'lat', 'lon')
- grad_tokens: bfloat16 [2, 24, 512, 384], P(None, 'lat', 'lon')
- grad_qkv: float32 [2, 512, 1536], P(None, None, ('lat', 'lon'))
- grad_proj: float32 [2, 512, 512], P(None, None, ('lat', 'lon'))
- grad_up: float32 [2, 512, 2048], P(None, None, ('lat', 'lon'))
- grad_down: float32 [2, 2048, 512], P(None, None, ('lat', 'lon'))
All inputs are finite; a program needn't handle non-finite values.
Results may differ from a plain program's by a relative error of at most 0.024.
Values may be sent and summed in bfloat16 or wider, within the bound.
A program may use at most 192 MiB of HBM per device.

v0:
```python
import jax
import jax.numpy as jnp
from jax import lax
from jax.sharding import PartitionSpec as P

HEADS = 16
WLAT = 6
WLON = 12


NORM_EPS = 1e-05


def from_behind(value, axis, steps):
    count = lax.axis_size(axis)
    pairs = [(source, (source + steps) % count) for source in range(count)]
    return lax.ppermute(value, axis, pairs)


def layer_norm(features):
    average = jnp.mean(features, -1, keepdims=True)
    centred = features - average
    variance = jnp.mean(centred * centred, -1, keepdims=True)
    return centred * lax.rsqrt(variance + NORM_EPS)


def product(pattern, former, latter):
    return jnp.einsum(pattern, former, latter, preferred_element_type=jnp.float32)


def window_block(tokens, extras, layer, pair_mask):
    w_qkv, w_proj, w_up, w_down = layer
    groups, window_len, channels = tokens.shape
    head_size = channels // HEADS
    normed = layer_norm(tokens).astype(jnp.bfloat16)
    projected = (product("gtc,cd->gtd", normed, w_qkv) + extras[0]).astype(jnp.bfloat16)
    queries = projected[..., :channels].reshape(groups, window_len, HEADS, head_size)
    key_vecs = projected[..., channels : 2 * channels].reshape(groups, window_len, HEADS, head_size)
    value_vecs = projected[..., 2 * channels :].reshape(groups, window_len, HEADS, head_size)
    scores = product("gthd,gshd->ghts", queries, key_vecs) * head_size ** (-0.5)
    exped = jnp.exp(scores) * pair_mask[:, None]
    probabilities = (exped / jnp.sum(exped, -1, keepdims=True)).astype(jnp.bfloat16)
    attended = product("ghts,gshd->gthd", probabilities, value_vecs)
    attended = attended.reshape(groups, window_len, channels).astype(jnp.bfloat16)
    middle = tokens + product("gtc,cd->gtd", attended, w_proj) + extras[1]
    normed_two = layer_norm(middle).astype(jnp.bfloat16)
    hidden = jax.nn.gelu(
        product("gtc,cf->gtf", normed_two, w_up) + extras[2], approximate=False
    ).astype(jnp.bfloat16)
    result = middle + product("gtf,fc->gtc", hidden, w_down) + extras[3]
    return (result, (normed, attended, normed_two, hidden))


def make_extras(tokens, layer):
    groups, window_len, channels = tokens.shape
    hidden_units = layer[2].shape[1]
    return (
        jnp.zeros((groups, window_len, 3 * channels), jnp.float32),
        jnp.zeros((groups, window_len, channels), jnp.float32),
        jnp.zeros((groups, window_len, hidden_units), jnp.float32),
        jnp.zeros((groups, window_len, channels), jnp.float32),
    )


def weight_grads(saved, extras_ct):
    return tuple(
        (
            product("gtc,gtd->cd", saved[index], extras_ct[index].astype(jnp.bfloat16))
            for index in range(4)
        )
    )


def to_windows(grid):
    levels, rows, cols, depth = grid.shape
    split = grid.reshape(levels, rows // WLAT, WLAT, cols // WLON, WLON, depth)
    split = split.transpose(1, 3, 0, 2, 4, 5)
    return split.reshape(rows // WLAT * (cols // WLON), levels * WLAT * WLON, depth)


def from_windows(blocks, levels, rows, cols):
    depth = blocks.shape[-1]
    split = blocks.reshape(rows // WLAT, cols // WLON, levels, WLAT, WLON, depth)
    return split.transpose(2, 0, 3, 1, 4, 5).reshape(levels, rows, cols, depth)


def window_mask(row_ids, total_rows, levels, cols, shifted):
    if shifted:
        labels = jnp.where(
            row_ids < total_rows - WLAT, 0.0, jnp.where(row_ids < total_rows - WLAT // 2, 1.0, 2.0)
        )
    else:
        labels = jnp.zeros(row_ids.shape, jnp.float32)
    label_grid = jnp.broadcast_to(
        labels.astype(jnp.float32)[None, :, None, None], (levels, row_ids.shape[0], cols, 1)
    )
    flat = to_windows(label_grid)[..., 0]
    return (flat[:, :, None] == flat[:, None, :]).astype(jnp.float32)


def roll_grid(grid, sign):
    cols = grid.shape[2]
    cut = WLON // 2 if sign > 0 else cols - WLON // 2
    leading = grid[:, :, :cut]
    trailing = grid[:, :, cut:]
    arrived = from_behind(leading if sign > 0 else trailing, "lon", -sign)
    grid = jnp.concatenate((trailing, arrived) if sign > 0 else (arrived, leading), 2)
    rows = grid.shape[1]
    cut = WLAT // 2 if sign > 0 else rows - WLAT // 2
    leading = grid[:, :cut]
    trailing = grid[:, cut:]
    arrived = from_behind(leading if sign > 0 else trailing, "lat", -sign)
    return jnp.concatenate((trailing, arrived) if sign > 0 else (arrived, leading), 1)


def forward_layer(grid, layer, masks):
    blocks = to_windows(grid.astype(jnp.float32))

    def local(values_in, extras):
        return window_block(values_in, extras, layer, masks)

    return jax.vjp(local, blocks, make_extras(blocks, layer), has_aux=True)


def on_device(encoded, upstream, w_qkv, w_proj, w_up, w_down):
    arrived = lax.all_to_all(encoded, "lon", split_axis=3, concat_axis=2, tiled=True)
    grid = jnp.transpose(arrived, (0, 1, 3, 2))
    levels, rows, cols, channels = grid.shape
    total_rows = rows * lax.axis_size("lat")
    row_ids = lax.axis_index("lat") * rows + jnp.arange(rows, dtype=jnp.int32)
    plain_mask = window_mask(row_ids, total_rows, levels, cols, False)
    shift_mask = window_mask(row_ids, total_rows, levels, cols, True)
    layer_one = (w_qkv[0], w_proj[0], w_up[0], w_down[0])
    layer_two = (w_qkv[1], w_proj[1], w_up[1], w_down[1])
    out_one, pull_one, saved_one = forward_layer(grid, layer_one, plain_mask)
    first = from_windows(out_one, levels, rows, cols).astype(jnp.bfloat16)
    rolled = roll_grid(first, 1)
    out_two, pull_two, saved_two = forward_layer(rolled, layer_two, shift_mask)
    mixed = roll_grid(from_windows(out_two, levels, rows, cols).astype(jnp.bfloat16), -1)
    back = roll_grid(upstream, 1)
    d_second, ext_two = pull_two(to_windows(back.astype(jnp.float32)))
    grads_two = weight_grads(saved_two, ext_two)
    g_mid = roll_grid(from_windows(d_second, levels, rows, cols).astype(jnp.bfloat16), -1)
    d_first, ext_one = pull_one(to_windows(g_mid.astype(jnp.float32)))
    grads_one = weight_grads(saved_one, ext_one)
    grad_grid = from_windows(d_first, levels, rows, cols).astype(jnp.bfloat16)
    leaving = lax.all_to_all(
        jnp.transpose(grad_grid, (0, 1, 3, 2)), "lon", split_axis=2, concat_axis=3, tiled=True
    )
    stacked = tuple((jnp.stack([grads_one[index], grads_two[index]]) for index in range(4)))
    shares = (
        lax.psum_scatter(stacked[0], ("lat", "lon"), scatter_dimension=2, tiled=True),
        lax.psum_scatter(stacked[1], ("lat", "lon"), scatter_dimension=2, tiled=True),
        lax.psum_scatter(stacked[2], ("lat", "lon"), scatter_dimension=2, tiled=True),
        lax.psum_scatter(stacked[3], ("lat", "lon"), scatter_dimension=2, tiled=True),
    )
    return (mixed, leaving, shares[0], shares[1], shares[2], shares[3])


def solution(mesh):
    return jax.shard_map(
        on_device,
        mesh=mesh,
        in_specs=(P(None, "lat", "lon", None), P(None, "lat", "lon", None), P(), P(), P(), P()),
        out_specs=(
            P(None, "lat", "lon", None),
            P(None, "lat", "lon", None),
            P(None, None, ("lat", "lon")),
            P(None, None, ("lat", "lon")),
            P(None, None, ("lat", "lon")),
            P(None, None, ("lat", "lon")),
        ),
        check_vma=False,
    )
```

profile of v0, /device:TPU:1, one launch (start us, length us, event | category | flops | bytes accessed | tf_op | source)
XLA Modules:
  0.0 471.4 jit_solution(12813735044961895759)
XLA Ops:
  7.2 2.1 copy.144
  9.3 1.9 reshape.1044
  11.2 9.8 %all-to-all-start = ((bf16[32,2,1152]{2,1,0:T(2,128)(2,1)}), bf16[32,2,1152]{2,1,0:T(2,128)(2,1)S(1)}, u32[]{:S(2)}, u32[]{:S(2)}) async-start(bf16[32,2,1152]{2,1,0:T(2,128)(2,1)} %reshape.1044), calls=%async_computation | async-start | bytes 294912 | tf_op jit(solution)/shard_map/all_to_all | solution.py:126
  21.2 5.6 %collective-permute-start.4 = (bf16[2,6,6,512]{3,0,2,1:T(2,128)(2,1)S(1)}, bf16[2,6,6,512]{3,0,2,1:T(2,128)(2,1)S(1)}, u32[]{:S(2)}, u32[]{:S(2)}) collective-permute-start(bf16[2,6,6,512]{3,0,2,1:T(2,128)(2,1)S(1)} %get-tuple-element.69), channel_id=1, source_target_pairs={{0,31},{1,0},{2,1},{3,2},{4,3},{5,4},{6,5},{7,6},{8,7},{9,8},{10,9... | collective-permute-start | bytes 221192 | tf_op jit(solution)/shard_map/ppermute | solution.py:17
  29.0 2.2 collective-permute-start.5
  31.3 1.5 reshape.1045
  33.8 5.0 %reshape.1043 = f32[2,6,16,32,12]{4,3,2,1,0:T(8,128)} reshape(bf16[2,6,16,384]{3,2,1,0:T(8,128)(2,1)S(1)} %copy.145) | data formatting | bytes 442368 | tf_op jit(solution)/shard_map/convert_element_type | solution.py:117
  38.8 4.5 copy.146
  43.3 1.2 reshape.1042
  47.4 1.8 fusion.13
  54.1 4.0 multiply_convert_fusion.1
  60.1 1.6 convert_element_type.410
  62.8 6.4 %collective-permute-start = (bf16[2,6,6,512]{3,2,1,0:T(8,128)(2,1)S(1)}, bf16[2,6,6,512]{3,2,1,0:T(8,128)(2,1)S(1)}, u32[]{:S(2)}, u32[]{:S(2)}) collective-permute-start(bf16[2,6,6,512]{3,2,1,0:T(8,128)(2,1)S(1)} %get-tuple-element.65), channel_id=1, source_target_pairs={{0,31},{1,0},{2,1},{3,2},{4,3},{5,4},{6,5},{7,6},{8,7},{9,8},{10,9... | collective-permute-start | bytes 221192 | tf_op jit(solution)/shard_map/ppermute | solution.py:17
  69.8 1.6 collective-permute-done
  75.1 1.6 concatenate.34
  76.7 1.6 collective-permute-done.1
  78.4 1.7 maximum_convert_fusion
  80.1 1.7 reshape.1039
  81.8 1.8 reshape.1040
  83.6 1.7 reshape.1041
  87.0 1.3 div.136
  90.0 2.0 fusion.14
  92.8 1.8 copy.160
  94.5 1.8 copy.161
  96.3 1.8 copy.162
  98.1 1.9 fusion.44
  103.9 3.7 multiply_convert_fusion
  111.5 1.8 copy.165
  113.3 2.8 fusion.7
  120.7 2.4 convolution_bitcast_fusion
  123.1 3.0 convolution_bitcast_fusion.4
  127.2 1.6 convert_element_type.452
  129.9 4.0 convolution_bitcast_fusion.2
  133.9 5.6 %collective-permute-done.6 = bf16[2,6,6,512]{3,2,1,0:T(8,128)(2,1)S(1)} collective-permute-done((bf16[2,6,6,512]{3,2,1,0:T(8,128)(2,1)S(1)}, bf16[2,6,6,512]{3,2,1,0:T(8,128)(2,1)S(1)}, u32[]{:S(2)}, u32[]{:S(2)}) %collective-permute-start.6) | collective-permute-done | bytes 73760 | tf_op jit(solution)/shard_map/ppermute | solution.py:17
  139.5 1.6 collective-permute-start.7
  141.1 1.4 convolution_bitcast_fusion.6
  143.5 1.6 concatenate.37
  145.1 3.4 multiply_add_fusion
  151.8 1.7 copy.169
  153.5 1.7 fusion.12
  158.5 1.4 convolution_bitcast_fusion.7
  159.8 2.8 convolution_bitcast_fusion.5
  162.7 2.7 convolution_bitcast_fusion.3
  167.3 3.1 pad_maximum_fusion.2
  170.4 10.3 %copy.176 = f32[2,512,1536]{1,0,2:T(2,128)} copy(f32[2,512,1536]{2,1,0:T(8,128)} %pad_maximum_fusion.2) | data formatting | bytes 12582912 | tf_op jit(solution)/shard_map/stack | solution.py:150
  180.7 1.4 pad_maximum_fusion.3
  182.1 2.5 copy.177
  184.6 7.9 %pad_maximum_fusion = f32[2,512,2048]{2,1,0:T(8,128)} fusion(f32[1,512,2048]{2,1,0:T(8,128)} %convolution_bitcast_fusion.4, f32[1,512,2048]{2,1,0:T(8,128)} %convolution_bitcast_fusion.5), kind=kLoop, calls=%fused_computation | loop fusion | flops 2097152 | bytes 16777216 | tf_op jit(solution)/shard_map/stack | solution.py:150
  192.4 13.2 %copy.178 = f32[2,512,2048]{1,0,2:T(2,128)} copy(f32[2,512,2048]{2,1,0:T(8,128)} %pad_maximum_fusion) | data formatting | bytes 16777216 | tf_op jit(solution)/shard_map/stack | solution.py:150
  205.6 7.8 %pad_maximum_fusion.1 = f32[2,2048,512]{2,1,0:T(8,128)} fusion(f32[1,2048,512]{2,1,0:T(8,128)} %convolution_bitcast_fusion.2, f32[1,2048,512]{2,1,0:T(8,128)} %convolution_bitcast_fusion.3), kind=kLoop, calls=%fused_computation.1 | loop fusion | flops 2097152 | bytes 16777216 | tf_op jit(solution)/shard_map/stack | solution.py:150
  213.4 13.4 %copy.179 = f32[2,2048,512]{1,0,2:T(2,128)} copy(f32[2,2048,512]{2,1,0:T(8,128)} %pad_maximum_fusion.1) | data formatting | bytes 16777216 | tf_op jit(solution)/shard_map/stack | solution.py:150
  228.0 2.2 fusion.71
  230.3 7.8 %collective-permute-done.2 = bf16[2,6,6,512]{3,2,1,0:T(8,128)(2,1)S(1)} collective-permute-done((bf16[2,6,6,512]{3,2,1,0:T(8,128)(2,1)S(1)}, bf16[2,6,6,512]{3,2,1,0:T(8,128)(2,1)S(1)}, u32[]{:S(2)}, u32[]{:S(2)}) %collective-permute-start.2) | collective-permute-done | bytes 73760 | tf_op jit(solution)/shard_map/ppermute | solution.py:17
  238.2 5.5 %collective-permute-start.3 = (bf16[2,3,12,512]{3,2,1,0:T(8,128)(2,1)S(1)}, bf16[2,3,12,512]{3,2,1,0:T(8,128)(2,1)S(1)}, u32[]{:S(2)}, u32[]{:S(2)}) collective-permute-start(bf16[2,3,12,512]{3,2,1,0:T(8,128)(2,1)S(1)} %fusion.122), channel_id=1, source_target_pairs={{0,32},{32,64},{64,96},{96,0},{1,33},{33,65},{65,97},{97,1},{2,34}... | collective-permute-start | bytes 221192 | tf_op jit(solution)/shard_map/ppermute | solution.py:17
  243.7 2.3 multiply_reduce_fusion
  246.4 1.7 copy.173
  248.1 3.9 reshape.1046
  251.9 3.9 all-to-all-start.1
  256.7 7.9 %all-to-all-done.1 = bf16[32,2,1152]{2,1,0:T(2,128)(2,1)S(1)} async-done(((bf16[32,2,1152]{2,1,0:T(2,128)(2,1)}), bf16[32,2,1152]{2,1,0:T(2,128)(2,1)S(1)}, u32[]{:S(2)}, u32[]{:S(2)}) %all-to-all-start.1) | async-done | bytes 147488 | tf_op jit(solution)/shard_map/all_to_all | solution.py:147
  264.5 3.6 reshape.1047
  268.2 2.2 copy.200
  270.3 4.5 all_to_all.24
  274.8 183.7 %all-reduce.13.cloned.1.call-done = (f32[2,512,1536]{1,0,2:T(2,128)}, f32[2,512,512]{1,0,2:T(2,128)}, f32[2,512,2048]{1,0,2:T(2,128)}, f32[2,2048,512]{1,0,2:T(2,128)}) async-done(((f32[2,512,1536]{1,0,2:T(2,128)}, f32[2,512,512]{1,0,2:T(2,128)}, f32[2,512,2048]{1,0,2:T(2,128)}, f32[2,2048,512]{1,0,2:T(2,128)}), (f32[2,512,1536]{1,0,2:T(2,128)}, f32[2,512,512]{1,0,2:T(2,128)}, f32[2,512,2048]{1,0,2:T(2,128)}, ...) | async-done | bytes 25165840
  462.9 1.4 constant_dynamic-slice_fusion.3
  (300 shorter events, 52.9 us)
Async XLA Ops:
  9.2 11.8 %copy-start.64 = (bf16[2,6,12,512]{3,0,2,1:T(2,128)(2,1)S(1)}, bf16[2,6,12,512]{3,0,2,1:T(2,128)(2,1)}, u32[]{:S(2)}) copy-start(bf16[2,6,12,512]{3,0,2,1:T(2,128)(2,1)} %param.7) | copy-start | bytes 442372
  11.2 20.1 %all-to-all-start = ((bf16[32,2,1152]{2,1,0:T(2,128)(2,1)}), bf16[32,2,1152]{2,1,0:T(2,128)(2,1)S(1)}, u32[]{:S(2)}, u32[]{:S(2)}) async-start(bf16[32,2,1152]{2,1,0:T(2,128)(2,1)} %reshape.1044), calls=%async_computation | async-start | bytes 294912 | tf_op jit(solution)/shard_map/all_to_all | solution.py:126
  21.0 437.5 %all-reduce.13.cloned.1.call-start = ((), (), s32[]{:S(2)}) async-start(), calls=%async_computation.2 | async-start | bytes 50331648
  21.2 7.0 %collective-permute-start.4 = (bf16[2,6,6,512]{3,0,2,1:T(2,128)(2,1)S(1)}, bf16[2,6,6,512]{3,0,2,1:T(2,128)(2,1)S(1)}, u32[]{:S(2)}, u32[]{:S(2)}) collective-permute-start(bf16[2,6,6,512]{3,0,2,1:T(2,128)(2,1)S(1)} %get-tuple-element.69), channel_id=1, source_target_pairs={{0,31},{1,0},{2,1},{3,2},{4,3},{5,4},{6,5},{7,6},{8,7},{9,8},{10,9... | collective-permute-start | bytes 221192 | tf_op jit(solution)/shard_map/ppermute | solution.py:17
  29.0 44.3 %collective-permute-start.5 = (bf16[2,3,12,512]{3,0,2,1:T(2,128)(2,1)}, bf16[2,3,12,512]{3,0,2,1:T(2,128)(2,1)}, u32[]{:S(2)}, u32[]{:S(2)}) collective-permute-start(bf16[2,3,12,512]{3,0,2,1:T(2,128)(2,1)} %get-tuple-element.67), channel_id=1, source_target_pairs={{0,96},{32,0},{64,32},{96,64},{1,97},{33,1},{65,33},{97,65},{2,98}... | collective-permute-start | bytes 221192 | tf_op jit(solution)/shard_map/ppermute | solution.py:17
  45.4 3.9 copy-start.38
  50.5 3.6 copy-start.93
  52.8 5.3 %copy-start.32 = (bf16[16,32,144]{2,1,0:T(8,128)(2,1)}, bf16[16,32,144]{2,1,0:T(8,128)(2,1)S(1)}, u32[]{:S(2)}) copy-start(bf16[16,32,144]{2,1,0:T(8,128)(2,1)S(1)} %convolution_convert_fusion.13) | copy-start | bytes 442372
  53.3 4.8 %copy-start.5 = (f32[144,512]{1,0:T(8,128)}, f32[144,512]{1,0:T(8,128)S(1)}, u32[]{:S(2)}) copy-start(f32[144,512]{1,0:T(8,128)S(1)} %get-tuple-element.73) | copy-start | bytes 884740
  53.3 4.8 %copy-start.65 = (f32[144]{0:T(256)}, f32[144]{0:T(256)S(1)}, u32[]{:S(2)}) copy-start(f32[144]{0:T(256)S(1)} %broadcast_multiply_fusion.3) | copy-start | bytes 1732
  54.1 4.0 copy-start.76
  54.1 4.9 %copy-start.96 = (bf16[2,2048,512]{2,1,0:T(8,128)(2,1)S(1)}, bf16[2,2048,512]{2,1,0:T(8,128)(2,1)}, u32[]{:S(2)}) copy-start(bf16[2,2048,512]{2,1,0:T(8,128)(2,1)} %param.11) | copy-start | bytes 12582916
  62.8 8.6 %collective-permute-start = (bf16[2,6,6,512]{3,2,1,0:T(8,128)(2,1)S(1)}, bf16[2,6,6,512]{3,2,1,0:T(8,128)(2,1)S(1)}, u32[]{:S(2)}, u32[]{:S(2)}) collective-permute-start(bf16[2,6,6,512]{3,2,1,0:T(8,128)(2,1)S(1)} %get-tuple-element.65), channel_id=1, source_target_pairs={{0,31},{1,0},{2,1},{3,2},{4,3},{5,4},{6,5},{7,6},{8,7},{9,8},{10,9... | collective-permute-start | bytes 221192 | tf_op jit(solution)/shard_map/ppermute | solution.py:17
  72.1 6.2 %collective-permute-start.1 = (bf16[2,3,12,512]{3,2,1,0:T(8,128)(2,1)}, bf16[2,3,12,512]{3,2,1,0:T(8,128)(2,1)}, u32[]{:S(2)}, u32[]{:S(2)}) collective-permute-start(bf16[2,3,12,512]{3,2,1,0:T(8,128)(2,1)} %get-tuple-element.63), channel_id=1, source_target_pairs={{0,96},{32,0},{64,32},{96,64},{1,97},{33,1},{65,33},{97,65},{2,98}... | collective-permute-start | bytes 221192 | tf_op jit(solution)/shard_map/ppermute | solution.py:17
  90.0 2.8 copy-start.91
  98.1 2.7 copy-start.36
  98.1 5.8 %copy-start.94 = (bf16[2,512,2048]{2,1,0:T(8,128)(2,1)S(1)}, bf16[2,512,2048]{2,1,0:T(8,128)(2,1)}, u32[]{:S(2)}) copy-start(bf16[2,512,2048]{2,1,0:T(8,128)(2,1)} %param.10) | copy-start | bytes 12582916
  101.4 2.2 copy-start.1
  102.1 5.5 %copy-start.34 = (bf16[16,32,144]{2,1,0:T(8,128)(2,1)}, bf16[16,32,144]{2,1,0:T(8,128)(2,1)S(1)}, u32[]{:S(2)}) copy-start(bf16[16,32,144]{2,1,0:T(8,128)(2,1)S(1)} %convolution_convert_fusion.12) | copy-start | bytes 442372
  103.6 5.9 %copy-start.8 = (f32[144,512]{1,0:T(8,128)}, f32[144,512]{1,0:T(8,128)S(1)}, u32[]{:S(2)}) copy-start(f32[144,512]{1,0:T(8,128)S(1)} %get-tuple-element.78) | copy-start | bytes 884740
  103.7 5.9 %copy-start.73 = (f32[144]{0:T(256)}, f32[144]{0:T(256)S(1)}, u32[]{:S(2)}) copy-start(f32[144]{0:T(256)S(1)} %broadcast_multiply_fusion.2) | copy-start | bytes 1732
  103.9 5.7 %copy-start.79 = (f32[144]{0:T(256)}, f32[144]{0:T(256)S(1)}, u32[]{:S(2)}) copy-start(f32[144]{0:T(256)S(1)} %fusion.128) | copy-start | bytes 1732
  103.9 3.7 copy-start.21
  103.9 3.7 copy-start.97
  113.3 2.9 copy-start.4
  113.3 2.9 copy-start.37
  113.3 2.9 copy-start.42
  113.3 2.9 copy-start.63
  117.1 2.3 copy-start.98
  120.6 2.4 copy-start.9
  120.6 2.4 copy-start.55
  120.6 2.4 copy-start.74
  120.7 2.4 copy-start.80
  123.1 3.0 copy-start.84
  123.1 3.3 copy-start.15
  123.1 3.3 copy-start.22
  123.1 3.3 copy-start.71
  129.8 9.7 %collective-permute-start.6 = (bf16[2,6,6,512]{3,2,1,0:T(8,128)(2,1)S(1)}, bf16[2,6,6,512]{3,2,1,0:T(8,128)(2,1)S(1)}, u32[]{:S(2)}, u32[]{:S(2)}) collective-permute-start(bf16[2,6,6,512]{3,2,1,0:T(8,128)(2,1)S(1)} %get-tuple-element.58), channel_id=1, source_target_pairs={{0,1},{1,2},{2,3},{3,4},{4,5},{5,6},{6,7},{7,8},{8,9},{9,10},{10,1... | collective-permute-start | bytes 221192 | tf_op jit(solution)/shard_map/ppermute | solution.py:17
  129.9 11.2 %copy-start.16 = (f32[144,512]{1,0:T(8,128)S(1)}, f32[144,512]{1,0:T(8,128)}, u32[]{:S(2)}) copy-start(f32[144,512]{1,0:T(8,128)} %copy-done.14) | copy-start | bytes 884740
  129.9 11.2 %copy-start.23 = (bf16[144,512]{1,0:T(8,128)(2,1)S(1)}, bf16[144,512]{1,0:T(8,128)(2,1)}, u32[]{:S(2)}) copy-start(bf16[144,512]{1,0:T(8,128)(2,1)} %concatenate.34) | copy-start | bytes 442372
  129.9 11.2 %copy-start.35 = (bf16[16,32,144]{2,1,0:T(8,128)(2,1)S(1)}, bf16[16,32,144]{2,1,0:T(8,128)(2,1)}, u32[]{:S(2)}) copy-start(bf16[16,32,144]{2,1,0:T(8,128)(2,1)} %copy-done.34) | copy-start | bytes 442372
  129.9 11.2 %copy-start.72 = (f32[144]{0:T(256)S(1)}, f32[144]{0:T(256)}, u32[]{:S(2)}) copy-start(f32[144]{0:T(256)} %copy-done.70) | copy-start | bytes 1732
  139.5 3.2 collective-permute-start.7
  145.1 3.4 copy-start.6
  145.1 3.4 copy-start.66
  145.1 3.7 copy-start.95
  148.8 2.0 copy-start.19
  156.2 9.2 %copy-start.58 = (bf16[16,144,32]{1,2,0:T(8,128)(2,1)}, bf16[16,144,32]{1,2,0:T(8,128)(2,1)S(1)}, u32[]{:S(2)}) copy-start(bf16[16,144,32]{1,2,0:T(8,128)(2,1)S(1)} %convolution_convert_fusion.6) | copy-start | bytes 442372
  157.2 8.2 %copy-start.60 = (bf16[16,144,32]{1,2,0:T(8,128)(2,1)}, bf16[16,144,32]{1,2,0:T(8,128)(2,1)S(1)}, u32[]{:S(2)}) copy-start(bf16[16,144,32]{1,2,0:T(8,128)(2,1)S(1)} %convolution_convert_fusion.7) | copy-start | bytes 442372
  158.4 7.0 %copy-start.49 = (bf16[16,32,144]{2,1,0:T(8,128)(2,1)}, bf16[16,32,144]{2,1,0:T(8,128)(2,1)S(1)}, u32[]{:S(2)}) copy-start(bf16[16,32,144]{2,1,0:T(8,128)(2,1)S(1)} %convolution_convert_fusion.8) | copy-start | bytes 442372
  159.8 2.8 copy-start.52
  162.7 2.8 copy-start.39
  162.7 2.8 copy-start.88
  162.7 2.8 copy-start.90
  170.4 10.3 %copy-start.20 = (f32[1,512,512]{2,1,0:T(8,128)S(1)}, f32[1,512,512]{2,1,0:T(8,128)}, u32[]{:S(2)}) copy-start(f32[1,512,512]{2,1,0:T(8,128)} %convolution_bitcast_fusion.6) | copy-start | bytes 3145732
  228.0 15.6 %copy-start.27 = (f32[144,512]{1,0:T(8,128)S(1)}, f32[144,512]{1,0:T(8,128)}, u32[]{:S(2)}) copy-start(f32[144,512]{1,0:T(8,128)} %reshape_transpose_reshape.4) | copy-start | bytes 884740
  228.0 15.6 %copy-start.50 = (bf16[16,32,144]{2,1,0:T(8,128)(2,1)S(1)}, bf16[16,32,144]{2,1,0:T(8,128)(2,1)}, u32[]{:S(2)}) copy-start(bf16[16,32,144]{2,1,0:T(8,128)(2,1)} %copy-done.49) | copy-start | bytes 442372
  228.0 15.6 %copy-start.59 = (bf16[16,144,32]{1,2,0:T(8,128)(2,1)S(1)}, bf16[16,144,32]{1,2,0:T(8,128)(2,1)}, u32[]{:S(2)}) copy-start(bf16[16,144,32]{1,2,0:T(8,128)(2,1)} %copy-done.58) | copy-start | bytes 442372
  228.0 15.6 %copy-start.61 = (bf16[16,144,32]{1,2,0:T(8,128)(2,1)S(1)}, bf16[16,144,32]{1,2,0:T(8,128)(2,1)}, u32[]{:S(2)}) copy-start(bf16[16,144,32]{1,2,0:T(8,128)(2,1)} %copy-done.60) | copy-start | bytes 442372
  230.3 7.9 %collective-permute-start.2 = (bf16[2,6,6,512]{3,2,1,0:T(8,128)(2,1)S(1)}, bf16[2,6,6,512]{3,2,1,0:T(8,128)(2,1)S(1)}, u32[]{:S(2)}, u32[]{:S(2)}) collective-permute-start(bf16[2,6,6,512]{3,2,1,0:T(8,128)(2,1)S(1)} %get-tuple-element.60), channel_id=1, source_target_pairs={{0,1},{1,2},{2,3},{3,4},{4,5},{5,6},{6,7},{7,8},{8,9},{9,10},{10,1... | collective-permute-start | bytes 221192 | tf_op jit(solution)/shard_map/ppermute | solution.py:17
  238.2 7.8 %copy-start.86 = (f32[144]{0:T(256)S(1)}, f32[144]{0:T(256)}, u32[]{:S(2)}) copy-start(f32[144]{0:T(256)} %copy-done.85) | copy-start | bytes 1732
  238.2 8.0 %copy-start.13 = (f32[144,512]{1,0:T(8,128)S(1)}, f32[144,512]{1,0:T(8,128)}, u32[]{:S(2)}) copy-start(f32[144,512]{1,0:T(8,128)} %copy-done.11) | copy-start | bytes 884740
  238.2 17.6 %collective-permute-start.3 = (bf16[2,3,12,512]{3,2,1,0:T(8,128)(2,1)S(1)}, bf16[2,3,12,512]{3,2,1,0:T(8,128)(2,1)S(1)}, u32[]{:S(2)}, u32[]{:S(2)}) collective-permute-start(bf16[2,3,12,512]{3,2,1,0:T(8,128)(2,1)S(1)} %fusion.122), channel_id=1, source_target_pairs={{0,32},{32,64},{64,96},{96,0},{1,33},{33,65},{65,97},{97,1},{2,34}... | collective-permute-start | bytes 221192 | tf_op jit(solution)/shard_map/ppermute | solution.py:17
  251.9 12.6 %all-to-all-start.1 = ((bf16[32,2,1152]{2,1,0:T(2,128)(2,1)}), bf16[32,2,1152]{2,1,0:T(2,128)(2,1)S(1)}, u32[]{:S(2)}, u32[]{:S(2)}) async-start(bf16[32,2,1152]{2,1,0:T(2,128)(2,1)} %reshape.1046), calls=%async_computation.1 | async-start | bytes 294912 | tf_op jit(solution)/shard_map/all_to_all | solution.py:147
  (46 other events, 51.0 us)
Sparse Core Ops, SparseCore 0:
  227.0 231.4 all-reduce.12
where the time goes:
time: 477 us; the launch traced here: 471 us
  waiting for transfers between devices  209 us (44%)
  local copies, waits for them, and re-layouts  120 us (25%)
  matrix products  56.8 us (12%)
  starting transfers between devices  36.3 us (8%)
  other arithmetic  33.7 us (7%)
  between operations  15.4 us (3%)
    unnamed x2, waiting for transfers between devices  184 us
    dot_general x36, matrix products, product(): jnp.einsum(pattern, former, latter, preferred_element_type=jnp.float32)  56.8 us
    another operation x4, local copies, waits for them, and re-layouts, on_device(): jnp.stack([grads_one[index], grads_two[index]])  39.4 us
    unnamed x211, local copies, waits for them, and re-layouts  32.6 us
    ppermute x8, starting transfers between devices, from_behind(): return lax.ppermute(value, axis, pairs)  22.6 us
    another operation x4, other arithmetic, on_device(): jnp.stack([grads_one[index], grads_two[index]])  20.1 us
    ppermute x8, waiting for transfers between devices, from_behind(): return lax.ppermute(value, axis, pairs)  17.2 us
    convert_element_type x7, local copies, waits for them, and re-layouts, forward_layer(): blocks = to_windows(grid.astype(jnp.float32))  16.1 us
  transfers between devices with their start and end apart: 11, of which 8 were waited for; matrix products, arithmetic and copies ran while one was open for 12% of the time, Pallas kernels for 0%

commit v1 on v0

v1 whole, which is shorter than its diff:
```python
import functools

import jax
import jax.numpy as jnp
import numpy as np
from jax import lax
from jax.experimental import pallas as pl
from jax.experimental.pallas import tpu as pltpu
from jax.sharding import PartitionSpec as P

HEADS = 16
WLAT = 6
WLON = 12
LEV = 2
C = 512
FF = 2048
T = LEV * WLAT * WLON
QUAD = T // 4
SLOT = 48
NORM_EPS = 1e-05
MESH = pl.DeviceIdType.MESH
BF = jnp.bfloat16
F32 = jnp.float32


def quadrant_order():
    return [
        (l, 3 * a + r, 6 * b + c)
        for a in range(2)
        for b in range(2)
        for l in range(LEV)
        for r in range(3)
        for c in range(6)
    ]


def permutations():
    slots_of_natural = np.zeros((4 * SLOT, 12 * 16), np.float32)
    tokens_of_slots = np.zeros((T, 4 * SLOT), np.float32)
    for t, (l, r, c) in enumerate(quadrant_order()):
        slot = t // QUAD * SLOT + t % QUAD
        slots_of_natural[slot, (l * WLAT + r) * 16 + c] = 1
        tokens_of_slots[t, slot] = 1
    return slots_of_natural, tokens_of_slots


def nn(a, b):
    return lax.dot_general(a, b, (((1,), (0,)), ((), ())), preferred_element_type=F32)


def nt(a, b):
    return lax.dot_general(a, b, (((1,), (1,)), ((), ())), preferred_element_type=F32)


def tn(a, b):
    return lax.dot_general(a, b, (((0,), (0,)), ((), ())), preferred_element_type=F32)


def norm(x):
    centred = x - jnp.mean(x, -1, keepdims=True)
    rstd = lax.rsqrt(jnp.mean(centred * centred, -1, keepdims=True) + NORM_EPS)
    return centred * rstd, rstd


def norm_back(dn, nhat, rstd):
    return rstd * (
        dn - jnp.mean(dn, -1, keepdims=True) - nhat * jnp.mean(dn * nhat, -1, keepdims=True)
    )


def layers_kernel(
    grid_ref, up_ref, son_ref, tos_ref, wqkv_hbm, wproj_hbm, wup_hbm, wdown_hbm,
    mixed_ref, dgrid_ref, gqkv_hbm, gproj_hbm, gup_hbm, gdown_hbm,
    wqkv, wproj, wup, wdown, wsem,
    nat, send, recv, send_sem, recv_sem,
    xs, n1h, n1, r1, us, ps, att, n2h, n2, r2, gp, hs, acc, eq, ep, eu, ed, dab,
    gqkv, gproj, gup, gdown, gsem,
):
    i, j = lax.axis_index("lat"), lax.axis_index("lon")
    nlat, nlon = lax.axis_size("lat"), lax.axis_size("lon")

    def device(di, dj):
        return (lax.rem(i + di + nlat, nlat), lax.rem(j + dj + nlon, nlon))

    weights = ((wqkv_hbm, wqkv), (wproj_hbm, wproj), (wup_hbm, wup), (wdown_hbm, wdown))
    fetches = []
    for k in range(2):
        for w, (src, dst) in enumerate(weights):
            fetch = pltpu.make_async_copy(src.at[k], dst.at[k], wsem.at[k, w])
            fetch.start()
            fetches.append(fetch)

    barrier = pltpu.get_barrier_semaphore()
    offsets = ((0, 1), (1, 0), (1, 1), (0, -1), (-1, 0), (-1, -1))
    for di, dj in offsets:
        pl.semaphore_signal(barrier, inc=1, device_id=device(di, dj), device_id_type=MESH)
    pl.semaphore_wait(barrier, len(offsets))

    def exchange(event, forward):
        copies = []
        for q in range(4):
            a, b = q // 2, q % 2
            di, dj = (a - 1, b - 1) if forward else (a, b)
            if (di, dj) == (0, 0):
                recv[event, 3 - q] = send[event, q]
            else:
                copy = pltpu.make_async_remote_copy(
                    src_ref=send.at[event, q], dst_ref=recv.at[event, 3 - q],
                    send_sem=send_sem.at[event, q], recv_sem=recv_sem.at[event, 3 - q],
                    device_id=device(di, dj), device_id_type=MESH,
                )
                copy.start()
                copies.append(copy)
        return copies

    def finish(copies):
        for copy in copies:
            copy.wait()

    def put(event, tokens):
        send[event] = tn(tos_ref[...], tokens).astype(BF).reshape(4, SLOT, C)

    def got(event):
        return nn(tos_ref[...], recv[event].reshape(4 * SLOT, C))

    nat[...] = jnp.zeros_like(nat)
    nat[:, 0:WLON, :] = up_ref[...]
    send[0] = nn(son_ref[...], nat[...].reshape(12 * 16, C)).astype(BF).reshape(4, SLOT, C)
    up_copies = exchange(0, True)

    lane = lax.broadcasted_iota(jnp.int32, (1, 128), 1)
    head_mask = [((lane >= 32 * s) & (lane < 32 * s + 32)).astype(BF) for s in range(4)]
    half_t = lax.broadcasted_iota(jnp.int32, (T, T), 0) < T // 2
    half_s = lax.broadcasted_iota(jnp.int32, (T, T), 1) < T // 2
    apart = jnp.where(half_t == half_s, 0.0, 1.0).astype(F32)
    last = jnp.where(i == nlat - 1, 1.0, 0.0).astype(F32)

    def forward(k, x):
        xs[k] = x
        nhat, rstd = norm(x)
        n1h[k] = nhat
        r1[k] = jnp.broadcast_to(rstd, (T, 128))
        n1[k] = nhat.astype(BF)
        fetches[4 * k].wait()

        @pl.loop(0, 3)
        def _(s):
            cols = pl.ds(pl.multiple_of(s * C, C), C)
            us[k, :, cols] = nn(n1[k], wqkv[k, :, cols]).astype(BF)

        @pl.loop(0, 4)
        def _(g):
            def part(w):
                return us[k, :, pl.ds(pl.multiple_of(w * C + g * 128, 128), 128)]

            q, key, v = part(0), part(1), part(2)
            total = jnp.zeros((T, 128), F32)
            for s in range(4):
                e = jnp.exp(nt(q * head_mask[s], key) * (32**-0.5))
                if k == 1:
                    e = e * (1.0 - last * apart)
                p = (e / jnp.sum(e, -1, keepdims=True)).astype(BF)
                ps[k, g * 4 + s] = p
                total += nn(p, v * head_mask[s])
            att[k, :, pl.ds(pl.multiple_of(g * 128, 128), 128)] = total.astype(BF)

        fetches[4 * k + 1].wait()
        m = xs[k] + nn(att[k], wproj[k])
        acc[...] = m
        nhat, rstd = norm(m)
        n2h[k] = nhat
        r2[k] = jnp.broadcast_to(rstd, (T, 128))
        n2[k] = nhat.astype(BF)
        fetches[4 * k + 2].wait()
        fetches[4 * k + 3].wait()

        @pl.loop(0, 4)
        def _(s):
            cols = pl.ds(pl.multiple_of(s * C, C), C)
            z = nn(n2[k], wup[k, :, cols])
            cdf = 0.5 * (1.0 + lax.erf(z * (2.0**-0.5)))
            gp[k, :, cols] = cdf + z * (jnp.exp(-0.5 * z * z) * ((2.0 * np.pi) ** -0.5))
            h = (z * cdf).astype(BF)
            hs[k, :, cols] = h
            acc[...] += nn(h, wdown[k, cols, :])

        return acc[...]

    def backward(k, ct):
        acc[...] = ct
        ed[...] = ct.astype(BF)

        @pl.loop(0, 4)
        def _(s):
            cols = pl.ds(pl.multiple_of(s * C, C), C)
            dh = nt(ed[...], wdown[k, cols, :]).astype(BF).astype(F32)
            eu[:, cols] = (dh * gp[k, :, cols]).astype(BF)

        dn2 = nt(eu[...], wup[k]).astype(BF).astype(F32)
        dm = acc[...] + norm_back(dn2, n2h[k], r2[k][:, 0:1])
        acc[...] = dm
        ep[...] = dm.astype(BF)
        dab[...] = nt(ep[...], wproj[k]).astype(BF)

        @pl.loop(0, 4)
        def _(g):
            def at(w):
                return pl.ds(pl.multiple_of(w * C + g * 128, 128), 128)

            q, key, v = us[k, :, at(0)], us[k, :, at(1)], us[k, :, at(2)]
            da = dab[:, at(0)]
            dq = jnp.zeros((T, 128), F32)
            dk = jnp.zeros((T, 128), F32)
            dv = jnp.zeros((T, 128), F32)
            for s in range(4):
                p = ps[k, g * 4 + s]
                dah = da * head_mask[s]
                dp = nt(dah, v).astype(BF).astype(F32)
                dv += tn(p, dah)
                pf = p.astype(F32)
                ds = pf * (dp - jnp.sum(dp * pf, -1, keepdims=True))
                ds = (ds * (32**-0.5)).astype(BF)
                dq += nn(ds, key * head_mask[s])
                dk += tn(ds, q * head_mask[s])
            eq[:, at(0)] = dq.astype(BF)
            eq[:, at(1)] = dk.astype(BF)
            eq[:, at(2)] = dv.astype(BF)

        dn1 = nt(eq[...], wqkv[k]).astype(BF).astype(F32)
        return acc[...] + norm_back(dn1, n1h[k], r1[k][:, 0:1])

    def weight_grads(k):
        @pl.loop(0, 3)
        def _(s):
            cols = pl.ds(pl.multiple_of(s * C, C), C)
            gqkv[k, cols, :] = tn(eq[:, cols], n1[k]).astype(BF)

        gproj[k] = tn(ep[...], att[k]).astype(BF)

        @pl.loop(0, 4)
        def _(s):
            cols = pl.ds(pl.multiple_of(s * C, C), C)
            gup[k, cols, :] = tn(eu[:, cols], n2[k]).astype(BF)
            gdown[k, :, cols] = tn(ed[...], hs[k, :, cols]).astype(BF)

        stores = []
        for w, (src, dst) in enumerate(
            ((gqkv, gqkv_hbm), (gproj, gproj_hbm), (gup, gup_hbm), (gdown, gdown_hbm))
        ):
            store = pltpu.make_async_copy(src.at[k], dst.at[k], gsem.at[k, w])
            store.start()
            stores.append(store)
        return stores

    first = forward(0, jnp.transpose(grid_ref[...].astype(F32)))
    put(1, first.astype(BF))
    finish(exchange(1, True))
    second = forward(1, got(1))
    put(2, second.astype(BF))
    mixed_copies = exchange(2, False)
    finish(up_copies)
    d_second = backward(1, got(0))
    put(3, d_second.astype(BF))
    mid_copies = exchange(3, False)
    stores = weight_grads(1)
    finish(mid_copies)
    d_first = backward(0, got(3))
    dgrid_ref[...] = jnp.transpose(d_first).astype(BF)
    stores += weight_grads(0)
    finish(mixed_copies)
    natural = tn(son_ref[...], recv[2].reshape(4 * SLOT, C)).astype(BF)
    mixed_ref[...] = natural.reshape(12, 16, C)[:, 0:WLON, :]
    finish(stores)


def layers(grid, upstream, w_qkv, w_proj, w_up, w_down):
    son, tos = permutations()
    vmem = pl.BlockSpec(memory_space=pltpu.VMEM)
    hbm = pl.BlockSpec(memory_space=pl.ANY)
    dma = pltpu.SemaphoreType.DMA
    V = pltpu.VMEM
    return pl.pallas_call(
        layers_kernel,
        out_shape=(
            jax.ShapeDtypeStruct((12, WLON, C), BF),
            jax.ShapeDtypeStruct((C, T), BF),
            jax.ShapeDtypeStruct((2, 3 * C, C), BF),
            jax.ShapeDtypeStruct((2, C, C), BF),
            jax.ShapeDtypeStruct((2, FF, C), BF),
            jax.ShapeDtypeStruct((2, C, FF), BF),
        ),
        in_specs=[vmem] * 4 + [hbm] * 4,
        out_specs=(vmem, vmem, hbm, hbm, hbm, hbm),
        scratch_shapes=[
            V((2, C, 3 * C), BF), V((2, C, C), BF), V((2, C, FF), BF), V((2, FF, C), BF),
            dma((2, 4)),
            V((12, 16, C), BF), V((4, 4, SLOT, C), BF), V((4, 4, SLOT, C), BF),
            dma((4, 4)), dma((4, 4)),
            V((2, T, C), F32), V((2, T, C), F32), V((2, T, C), BF), V((2, T, 128), F32),
            V((2, T, 3 * C), BF), V((2, HEADS, T, T), BF), V((2, T, C), BF),
            V((2, T, C), F32), V((2, T, C), BF), V((2, T, 128), F32),
            V((2, T, FF), F32), V((2, T, FF), BF), V((T, C), F32),
            V((T, 3 * C), BF), V((T, C), BF), V((T, FF), BF), V((T, C), BF), V((T, C), BF),
            V((2, 3 * C, C), BF), V((2, C, C), BF), V((2, FF, C), BF), V((2, C, FF), BF),
            dma((2, 4)),
        ],
        compiler_params=pltpu.CompilerParams(
            collective_id=0, has_side_effects=True, vmem_limit_bytes=60 * 2**20
        ),
    )(grid, upstream, jnp.asarray(son, BF), jnp.asarray(tos, BF), w_qkv, w_proj, w_up, w_down)


def on_device(encoded, upstream, w_qkv, w_proj, w_up, w_down):
    levels, rows, width, cols = encoded.shape
    nlon = cols // WLON
    pieces = encoded.reshape(levels, 2, 3, width, nlon, 2, 6)
    pieces = pieces.transpose(4, 3, 1, 5, 0, 2, 6).reshape(nlon * width, T)
    grid = lax.all_to_all(pieces, "lon", split_axis=0, concat_axis=0, tiled=True)
    up = upstream.reshape(levels * rows, WLON, C)
    mixed, dgrid, *grads = layers(grid, up, w_qkv, w_proj, w_up, w_down)
    leaving = lax.all_to_all(dgrid, "lon", split_axis=0, concat_axis=0, tiled=True)
    leaving = leaving.reshape(nlon, width, 2, 2, levels, 3, 6).transpose(4, 2, 5, 1, 0, 3, 6)
    shares = [
        lax.psum_scatter(g, ("lat", "lon"), scatter_dimension=1, tiled=True).astype(F32)
        for g in grads
    ]
    return (
        mixed.reshape(upstream.shape),
        leaving.reshape(encoded.shape),
        *[jnp.swapaxes(s, 1, 2) for s in shares],
    )


def solution(mesh):
    return jax.shard_map(
        on_device,
        mesh=mesh,
        in_specs=(P(None, "lat", "lon", None), P(None, "lat", "lon", None), P(), P(), P(), P()),
        out_specs=(
            P(None, "lat", "lon", None),
            P(None, "lat", "lon", None),
            P(None, None, ("lat", "lon")),
            P(None, None, ("lat", "lon")),
            P(None, None, ("lat", "lon")),
            P(None, None, ("lat", "lon")),
        ),
        check_vma=False,
    )
```

time: 477 us -> 904 us (1.90)
  the two profiles are of different devices: /device:TPU:1 before, /device:TPU:0 now
where the time goes in v1:
time: 904 us
  waiting for transfers between devices  801 us (89%)
  Pallas kernels  50.3 us (6%)
  local copies, waits for them, and re-layouts  19.4 us (2%)
  between operations  14.1 us (2%)
  starting transfers between devices  13.3 us (1%)
    reduce_scatter x1, waiting for transfers between devices, on_device(): lax.psum_scatter(g, ('lat', 'lon'), scatter_dimension=1, tiled=True)  641 us
    unnamed x3, waiting for transfers between devices  142 us
    pallas_call x1, Pallas kernels, layers(): pl.pallas_call(layers_kernel, out_shape=(jax.ShapeDtypeStruct((12, WLON,...  50.3 us
  transfers between devices with their start and end apart: 4, of which 4 were waited for; matrix products, arithmetic and copies ran while one was open for 1% of the time, Pallas kernels for 0%

profile of v1, /device:TPU:0, one launch (start us, length us, event | category | flops | bytes accessed | tf_op | source)
XLA Modules:
  0.0 903.6 jit_solution(5392253186712737732)
XLA Ops:
  7.2 0.0 copy-start.2
  7.2 3.0 copy.28
  10.2 0.9 copy.29
  11.1 1.4 copy.30
  12.5 9.3 %all-to-all-start = ((bf16[32,16,144]{2,1,0:T(8,128)(2,1)}), bf16[32,16,144]{2,1,0:T(8,128)(2,1)S(1)}, u32[]{:S(2)}, u32[]{:S(2)}) async-start(bf16[32,16,144]{2,1,0:T(8,128)(2,1)} %copy.30), calls=%async_computation | async-start | bytes 524288 | tf_op jit(solution)/shard_map/all_to_all | solution.py:318
  21.9 0.0 all-reduce.6.cloned.1.call-start
  21.9 0.0 copy-done.2
  21.9 0.7 copy.31
  22.6 8.4 all-to-all-done
  31.0 0.0 copy-start
  31.0 0.7 copy-done
  31.7 50.3 %shard_map.127 = (bf16[12,12,512]{2,1,0:T(8,128)(2,1)}, bf16[512,144]{1,0:T(8,128)(2,1)}, bf16[2,1536,512]{2,1,0:T(8,128)(2,1)}, bf16[2,512,512]{2,1,0:T(8,128)(...) custom-call(bf16[512,144]{1,0:T(8,128)(2,1)} %bitcast.28, bf16[12,12,512]{2,1,0:T(8,128)(2,1)} %bitcast.29, ...), custom_call_target="tpu_custom_call" | custom-call | tf_op jit(solution)/shard_map/pallas_call | solution.py:282
  82.0 7.9 copy.34
  89.9 0.0 all-reduce.6.cloned.1.call-update
  89.9 0.0 copy-start.1
  90.0 0.0 reduce-scatter.4.cloned.1.call-start
  90.0 0.7 reduce-scatter.4.cloned.1.call-update
  90.7 3.9 all-to-all-start.1
  94.6 0.0 copy-done.1
  94.6 0.8 copy.35
  95.4 9.9 %all-to-all-done.1 = bf16[32,16,144]{2,1,0:T(8,128)(2,1)S(1)} async-done(((bf16[32,16,144]{2,1,0:T(8,128)(2,1)}), bf16[32,16,144]{2,1,0:T(8,128)(2,1)S(1)}, u32[]{:S(2)}, u32[]{:S(2)}) %all-to-all-start.1) | async-done | bytes 147488 | tf_op jit(solution)/shard_map/all_to_all | solution.py:321
  105.4 0.6 copy.32
  106.0 0.9 copy.33
  106.9 2.4 copy.36
  109.3 141.0 %all-reduce.6.cloned.1.call-done = (bf16[2,1536,512]{2,0,1:T(2,128)(2,1)}, bf16[2,512,512]{2,1,0:T(8,128)(2,1)}, bf16[2,512,2048]{2,1,0:T(8,128)(2,1)}) async-done(((bf16[2,1536,512]{2,0,1:T(2,128)(2,1)}, bf16[2,512,512]{2,1,0:T(8,128)(2,1)}, bf16[2,512,2048]{2,1,0:T(8,128)(2,1)}), (bf16[2,1536,512]{2,0,1:T(2,128)(2,1)}, bf16[2,512,512]{2,1,0:T(8,128)(2,1)}, ...) | async-done | bytes 8388624
  250.3 1.3 convert_bitcast_fusion.3
  251.7 1.4 convert_bitcast_fusion.2
  253.0 1.5 convert_bitcast_fusion
  254.5 640.8 %reduce-scatter.4.cloned.1.call-done = bf16[2,16,512]{2,1,0:T(8,128)(2,1)} async-done(((bf16[2,2048,512]{2,1,0:T(8,128)(2,1)}), bf16[2,16,512]{2,1,0:T(8,128)(2,1)}) %reduce-scatter.4.cloned.1.call-update) | async-done | bytes 32784 | tf_op jit(solution)/shard_map/reduce_scatter | solution.py:324
  895.3 1.4 convert_bitcast_fusion.1
Async XLA Ops:
  7.2 14.8 %copy-start.2 = (bf16[2,6,12,512]{3,0,2,1:T(2,128)(2,1)S(1)}, bf16[2,6,12,512]{3,0,2,1:T(2,128)(2,1)}, u32[]{:S(2)}) copy-start(bf16[2,6,12,512]{3,0,2,1:T(2,128)(2,1)} %param.9) | copy-start | bytes 442372
  12.5 18.5 %all-to-all-start = ((bf16[32,16,144]{2,1,0:T(8,128)(2,1)}), bf16[32,16,144]{2,1,0:T(8,128)(2,1)S(1)}, u32[]{:S(2)}, u32[]{:S(2)}) async-start(bf16[32,16,144]{2,1,0:T(8,128)(2,1)} %copy.30), calls=%async_computation | async-start | bytes 524288 | tf_op jit(solution)/shard_map/all_to_all | solution.py:318
  21.9 228.5 %all-reduce.6.cloned.1.call-start = ((), (), s32[]{:S(2)}) async-start(), calls=%async_computation.4 | async-start | bytes 16777216
  31.0 0.7 copy-start
  89.9 4.7 copy-start.1
  90.0 805.4 %reduce-scatter.4.cloned.1.call-start = ((), (), s32[]{:S(2)}) async-start(), calls=%async_computation.3 | async-start | bytes 4227072 | tf_op jit(solution)/shard_map/reduce_scatter | solution.py:324
  90.7 14.7 %all-to-all-start.1 = ((bf16[32,16,144]{2,1,0:T(8,128)(2,1)}), bf16[32,16,144]{2,1,0:T(8,128)(2,1)S(1)}, u32[]{:S(2)}, u32[]{:S(2)}) async-start(bf16[32,16,144]{2,1,0:T(8,128)(2,1)} %bitcast.10), calls=%async_computation.1 | async-start | bytes 524288 | tf_op jit(solution)/shard_map/all_to_all | solution.py:321
Sparse Core Ops, SparseCore 0:
  90.1 160.2 all-reduce.5
  252.8 642.4 reduce-scatter.3

commit v2 on v1

--- a/solution.py
+++ b/solution.py
@@ -70,17 +70,28 @@
 
 def layers_kernel(
     grid_ref, up_ref, son_ref, tos_ref, wqkv_hbm, wproj_hbm, wup_hbm, wdown_hbm,
-    mixed_ref, dgrid_ref, gqkv_hbm, gproj_hbm, gup_hbm, gdown_hbm,
+    mixed_ref, dgrid_ref, grads_ref,
     wqkv, wproj, wup, wdown, wsem,
     nat, send, recv, send_sem, recv_sem,
     xs, n1h, n1, r1, us, ps, att, n2h, n2, r2, gp, hs, acc, eq, ep, eu, ed, dab,
-    gqkv, gproj, gup, gdown, gsem,
+    pn1, patt, pn2, phs, peq, pep, peu, ped, pair_send, pair_recv,
+    part, fwd, fsum, side, part2, fwd2, fsum2, side2, part3, side3, ring_send, ring_recv,
 ):
     i, j = lax.axis_index("lat"), lax.axis_index("lon")
     nlat, nlon = lax.axis_size("lat"), lax.axis_size("lon")
 
     def device(di, dj):
         return (lax.rem(i + di + nlat, nlat), lax.rem(j + dj + nlon, nlon))
+
+    core, z, y = lax.rem(i, 2), lax.rem(j, 4), j // 8
+    x = i // 2 * 2 + lax.rem(j // 4, 2)
+
+    def along(axis, steps):
+        at = {"x": x, "y": y, "z": z}
+        at[axis] = lax.rem(at[axis] + steps + 4, 4)
+        return (at["x"] // 2 * 2 + core, at["y"] * 8 + lax.rem(at["x"], 2) * 4 + at["z"])
+
+    partner = (i + 1 - 2 * core, j)
 
     weights = ((wqkv_hbm, wqkv), (wproj_hbm, wproj), (wup_hbm, wup), (wdown_hbm, wdown))
     fetches = []
@@ -92,9 +103,171 @@
 
     barrier = pltpu.get_barrier_semaphore()
     offsets = ((0, 1), (1, 0), (1, 1), (0, -1), (-1, 0), (-1, -1))
-    for di, dj in offsets:
-        pl.semaphore_signal(barrier, inc=1, device_id=device(di, dj), device_id_type=MESH)
-    pl.semaphore_wait(barrier, len(offsets))
+    greeted = [device(di, dj) for di, dj in offsets]
+    greeted += [along(axis, steps) for axis in "xyz" for steps in (1, 2, 3)] + [partner]
+    for other in greeted:
+        pl.semaphore_signal(barrier, inc=1, device_id=other, device_id_type=MESH)
+    pl.semaphore_wait(barrier, len(greeted))
+
+    def remote(src, dst, sems, index, to):
+        copy = pltpu.make_async_remote_copy(
+            src_ref=src, dst_ref=dst, send_sem=sems[0].at[index], recv_sem=sems[1].at[index],
+            device_id=to, device_id_type=MESH,
+        )
+        copy.start()
+        sent.append(copy)
+        return copy
+
+    sent = []
+    pairs = {}
+    wide = {"eq": 384, "ep": 128, "eu": 512, "ed": 128}
+    whole = {"n1": (n1, pn1), "att": (att, patt), "n2": (n2, pn2), "hs": (hs, phs)}
+    cut = {"eq": (eq, peq), "ep": (ep, pep), "eu": (eu, peu), "ed": (ed, ped)}
+
+    def columns(name, hi, owner):
+        width = wide[name]
+        return pl.ds(pl.multiple_of((2 * hi + owner) * width, width), width)
+
+    def give(k, name):
+        sems = (pair_send, pair_recv)
+        if name in whole:
+            src, dst = whole[name]
+            index = list(whole).index(name)
+            pairs[k, name] = [remote(src.at[k], dst.at[k], sems, (k, index), partner)]
+        else:
+            src, dst = cut[name]
+            index = 4 + 2 * list(cut).index(name)
+            pairs[k, name] = [
+                remote(src.at[k, :, columns(name, hi, 1 - core)], dst.at[k, hi], sems, (k, index + hi), partner)
+                for hi in range(2)
+            ]
+
+    def take(k, name):
+        for copy in pairs[k, name]:
+            copy.wait_recv()
+
+    orders = ("xyz", "zyx", "yxz")
+    rings = {}
+
+    def chunk(k, p, phase, t, half):
+        t = lax.rem(t + 4, 4)
+        if phase == 0:
+            return part.at[k, p, t, pl.ds(2 * half, 2)]
+        return part2.at[k, p, t, pl.ds(32 * half, 32)]
+
+    def ring_bufs(k, p, phase):
+        if phase == 0:
+            halves = [[side.at[k, p, s, pl.ds(2 * h, 2)] for h in range(2)] for s in range(2)]
+            return [fwd.at[k, p, s] for s in range(2)], [fsum.at[k, p, s] for s in range(2)], halves
+        halves = [[side2.at[k, p, s, pl.ds(32 * h, 32)] for h in range(2)] for s in range(2)]
+        return [fwd2.at[k, p, s] for s in range(2)], [fsum2.at[k, p, s] for s in range(2)], halves
+
+    def f32(ref):
+        return ref[...].astype(F32)
+
+    def ring_start(k, p, phase):
+        axis = orders[p][phase]
+        t = {"x": x, "y": y, "z": z}[axis]
+        after, before = along(axis, 1), along(axis, -1)
+        f, _, halves = ring_bufs(k, p, phase)
+        sems = (ring_send, ring_recv)
+        o = 6 * phase
+        rings[k, p, phase] = [
+            remote(chunk(k, p, phase, t + 2, 0), f[0], sems, (k, p, o), after),
+            remote(chunk(k, p, phase, t + 2, 1), f[1], sems, (k, p, o + 1), before),
+            remote(chunk(k, p, phase, t + 1, 1), halves[0][1], sems, (k, p, o + 2), after),
+            remote(chunk(k, p, phase, t - 1, 0), halves[1][0], sems, (k, p, o + 3), before),
+        ]
+
+    def ring_mid(k, p, phase):
+        axis = orders[p][phase]
+        t = {"x": x, "y": y, "z": z}[axis]
+        after, before = along(axis, 1), along(axis, -1)
+        f, fs, halves = ring_bufs(k, p, phase)
+        copies = rings[k, p, phase]
+        sems = (ring_send, ring_recv)
+        o = 6 * phase
+        copies[0].wait_recv()
+        fs[0][...] = (f32(f[0]) + f32(chunk(k, p, phase, t + 1, 0))).astype(BF)
+        copies.append(remote(fs[0], halves[0][0], sems, (k, p, o + 4), after))
+        copies[1].wait_recv()
+        fs[1][...] = (f32(f[1]) + f32(chunk(k, p, phase, t - 1, 1))).astype(BF)
+        copies.append(remote(fs[1], halves[1][1], sems, (k, p, o + 5), before))
+
+    def ring_end(k, p, phase):
+        axis = orders[p][phase]
+        t = {"x": x, "y": y, "z": z}[axis]
+        for copy in rings[k, p, phase][2:]:
+            copy.wait_recv()
+        if phase == 0:
+            total = f32(part.at[k, p, t]) + f32(side.at[k, p, 0]) + f32(side.at[k, p, 1])
+            part2[k, p] = total.astype(BF)
+            ring_start(k, p, 1)
+            return
+        total = f32(part2.at[k, p, t]) + f32(side2.at[k, p, 0]) + f32(side2.at[k, p, 1])
+        for s in range(4):
+            if p == 0:
+                rows = (total[12 * s : 12 * s + 12], total[48 + 4 * s : 52 + 4 * s])
+                rows = jnp.concatenate(rows, 0)
+            elif p == 1:
+                rows = total[16 * s : 16 * s + 16]
+            else:
+                rows = [total[16 * hb + 4 * s : 16 * hb + 4 * s + 4] for hb in range(4)]
+                rows = jnp.concatenate(rows, 0)
+            part3[k, p, s] = rows
+        axis = orders[p][2]
+        t = {"x": x, "y": y, "z": z}[axis]
+        rings[k, p, 2] = [
+            remote(
+                part3.at[k, p, lax.rem(t + s, 4)], side3.at[k, p, s - 1], (ring_send, ring_recv),
+                (k, p, 11 + s), along(axis, s),
+            )
+            for s in (1, 2, 3)
+        ]
+
+    def ring_last(k, p):
+        t = {"x": x, "y": y, "z": z}[orders[p][2]]
+        for copy in rings[k, p, 2]:
+            copy.wait_recv()
+        grads_ref[k, p] = part3[k, p, t] + side3[k, p, 0] + side3[k, p, 1] + side3[k, p, 2]
+
+    def both(k, name, hi, own, theirs):
+        src, dst = cut[name]
+        return tn(src[k, :, columns(name, hi, core)], own) + tn(dst[k, hi], theirs)
+
+    def grads_a(k):
+        for name in ("n1", "att", "ep", "eq"):
+            take(k, name)
+        for hi in range(2):
+            g = both(k, "eq", hi, n1[k], pn1[k]).astype(BF)
+            for at in range(8):
+                part[k, 0, 2 * hi + at % 2, at // 2, 0:48, :] = g[48 * at : 48 * at + 48]
+            g = both(k, "ep", hi, att[k], patt[k]).astype(BF)
+            for at in range(8):
+                part[k, 0, 2 * hi + at % 2, at // 2, 48:64, :] = g[16 * at : 16 * at + 16]
+        ring_start(k, 0, 0)
+
+    def grads_b(k):
+        for name in ("n2", "eu"):
+            take(k, name)
+        for hi in range(2):
+            g = both(k, "eu", hi, n2[k], pn2[k]).astype(BF)
+            for at in range(32):
+                row = (2 * hi + at // 4 % 2) * 16
+                part[k, 1, at % 4, at // 8, row : row + 16, :] = g[16 * at : 16 * at + 16]
+        ring_start(k, 1, 0)
+
+    def grads_c(k):
+        for name in ("hs", "ed"):
+            take(k, name)
+        for hi in range(2):
+            for hb in range(4):
+                cols = slice(hb * C, hb * C + C)
+                g = both(k, "ed", hi, hs[k, :, cols], phs[k, :, cols]).astype(BF)
+                for at in range(8):
+                    row = 16 * hb
+                    part[k, 2, at // 2, 2 * hi + at % 2, row : row + 16, :] = g[16 * at : 16 * at + 16]
+        ring_start(k, 2, 0)
 
     def exchange(event, forward):
         copies = []
@@ -141,6 +314,7 @@
         n1h[k] = nhat
         r1[k] = jnp.broadcast_to(rstd, (T, 128))
         n1[k] = nhat.astype(BF)
+        give(k, "n1")
         fetches[4 * k].wait()
 
         @pl.loop(0, 3)
@@ -164,6 +338,7 @@
                 total += nn(p, v * head_mask[s])
             att[k, :, pl.ds(pl.multiple_of(g * 128, 128), 128)] = total.astype(BF)
 
+        give(k, "att")
         fetches[4 * k + 1].wait()
         m = xs[k] + nn(att[k], wproj[k])
         acc[...] = m
@@ -171,6 +346,7 @@
         n2h[k] = nhat
         r2[k] = jnp.broadcast_to(rstd, (T, 128))
         n2[k] = nhat.astype(BF)
+        give(k, "n2")
         fetches[4 * k + 2].wait()
         fetches[4 * k + 3].wait()
 
@@ -184,26 +360,33 @@
             hs[k, :, cols] = h
             acc[...] += nn(h, wdown[k, cols, :])
 
+        give(k, "hs")
         return acc[...]
 
-    def backward(k, ct):
+    def backward(k, ct, after_up, after_proj, amid):
         acc[...] = ct
-        ed[...] = ct.astype(BF)
+        ed[k] = ct.astype(BF)
+        give(k, "ed")
 
         @pl.loop(0, 4)
         def _(s):
             cols = pl.ds(pl.multiple_of(s * C, C), C)
-            dh = nt(ed[...], wdown[k, cols, :]).astype(BF).astype(F32)
-            eu[:, cols] = (dh * gp[k, :, cols]).astype(BF)
-
-        dn2 = nt(eu[...], wup[k]).astype(BF).astype(F32)
+            dh = nt(ed[k], wdown[k, cols, :]).astype(BF).astype(F32)
+            eu[k, :, cols] = (dh * gp[k, :, cols]).astype(BF)
+
+        give(k, "eu")
+        after_up()
+        dn2 = nt(eu[k], wup[k]).astype(BF).astype(F32)
         dm = acc[...] + norm_back(dn2, n2h[k], r2[k][:, 0:1])
         acc[...] = dm
-        ep[...] = dm.astype(BF)
-        dab[...] = nt(ep[...], wproj[k]).astype(BF)
-
-        @pl.loop(0, 4)
-        def _(g):
+        ep[k] = dm.astype(BF)
+        give(k, "ep")
+        grads_c(k)
+        dab[...] = nt(ep[k], wproj[k]).astype(BF)
+        grads_b(k)
+        after_proj()
+
+        def heads(g):
             def at(w):
                 return pl.ds(pl.multiple_of(w * C + g * 128, 128), 128)
 
@@ -222,35 +405,21 @@
                 ds = (ds * (32**-0.5)).astype(BF)
                 dq += nn(ds, key * head_mask[s])
                 dk += tn(ds, q * head_mask[s])
-            eq[:, at(0)] = dq.astype(BF)
-            eq[:, at(1)] = dk.astype(BF)
-            eq[:, at(2)] = dv.astype(BF)
-
-        dn1 = nt(eq[...], wqkv[k]).astype(BF).astype(F32)
+            eq[k, :, at(0)] = dq.astype(BF)
+            eq[k, :, at(1)] = dk.astype(BF)
+            eq[k, :, at(2)] = dv.astype(BF)
+
+        pl.loop(0, 2)(heads)
+        amid()
+        pl.loop(2, 4)(heads)
+        give(k, "eq")
+
+    def backward_end(k):
+        dn1 = nt(eq[k], wqkv[k]).astype(BF).astype(F32)
         return acc[...] + norm_back(dn1, n1h[k], r1[k][:, 0:1])
 
-    def weight_grads(k):
-        @pl.loop(0, 3)
-        def _(s):
-            cols = pl.ds(pl.multiple_of(s * C, C), C)
-            gqkv[k, cols, :] = tn(eq[:, cols], n1[k]).astype(BF)
-
-        gproj[k] = tn(ep[...], att[k]).astype(BF)
-
-        @pl.loop(0, 4)
-        def _(s):
-            cols = pl.ds(pl.multiple_of(s * C, C), C)
-            gup[k, cols, :] = tn(eu[:, cols], n2[k]).astype(BF)
-            gdown[k, :, cols] = tn(ed[...], hs[k, :, cols]).astype(BF)
-
-        stores = []
-        for w, (src, dst) in enumerate(
-            ((gqkv, gqkv_hbm), (gproj, gproj_hbm), (gup, gup_hbm), (gdown, gdown_hbm))
-        ):
-            store = pltpu.make_async_copy(src.at[k], dst.at[k], gsem.at[k, w])
-            store.start()
-            stores.append(store)
-        return stores
+    def nothing():
+        pass
 
     first = forward(0, jnp.transpose(grid_ref[...].astype(F32)))
     put(1, first.astype(BF))
@@ -259,18 +428,61 @@
     put(2, second.astype(BF))
     mixed_copies = exchange(2, False)
     finish(up_copies)
-    d_second = backward(1, got(0))
+
+    def amid_one():
+        ring_mid(1, 2, 0)
+
+    backward(1, got(0), nothing, nothing, amid_one)
+    ring_mid(1, 1, 0)
+    d_second = backward_end(1)
     put(3, d_second.astype(BF))
     mid_copies = exchange(3, False)
-    stores = weight_grads(1)
+    ring_end(1, 2, 0)
+    grads_a(1)
+    ring_end(1, 1, 0)
+    ring_mid(1, 2, 1)
     finish(mid_copies)
-    d_first = backward(0, got(3))
+
+    def up_zero():
+        ring_mid(1, 0, 0)
+        ring_mid(1, 1, 1)
+        ring_end(1, 2, 1)
+
+    def proj_zero():
+        ring_end(1, 0, 0)
+        ring_end(1, 1, 1)
+        ring_last(1, 2)
+
+    def amid_zero():
+        ring_mid(1, 0, 1)
+        ring_mid(0, 2, 0)
+        ring_mid(0, 1, 0)
+        ring_last(1, 1)
+
+    backward(0, got(3), up_zero, proj_zero, amid_zero)
+    grads_a(0)
+    ring_end(1, 0, 1)
+    ring_end(0, 2, 0)
+    ring_end(0, 1, 0)
+    d_first = backward_end(0)
     dgrid_ref[...] = jnp.transpose(d_first).astype(BF)
-    stores += weight_grads(0)
+    ring_mid(0, 0, 0)
+    ring_mid(0, 2, 1)
+    ring_mid(0, 1, 1)
+    ring_last(1, 0)
     finish(mixed_copies)
     natural = tn(son_ref[...], recv[2].reshape(4 * SLOT, C)).astype(BF)
     mixed_ref[...] = natural.reshape(12, 16, C)[:, 0:WLON, :]
-    finish(stores)
+    ring_end(0, 0, 0)
+    ring_end(0, 2, 1)
+    ring_end(0, 1, 1)
+    ring_mid(0, 0, 1)
+    ring_last(0, 2)
+    ring_last(0, 1)
+    ring_end(0, 0, 1)
+    ring_last(0, 0)
+    for copy in sent:
+        copy.wait_send()
 
 
 def layers(grid, upstream, w_qkv, w_proj, w_up, w_down):
@@ -284,13 +496,10 @@
         out_shape=(
             jax.ShapeDtypeStruct((12, WLON, C), BF),
             jax.ShapeDtypeStruct((C, T), BF),
-            jax.ShapeDtypeStruct((2, 3 * C, C), BF),
-            jax.ShapeDtypeStruct((2, C, C), BF),
-            jax.ShapeDtypeStruct((2, FF, C), BF),
-            jax.ShapeDtypeStruct((2, C, FF), BF),
+            jax.ShapeDtypeStruct((2, 3, 16, C), F32),
         ),
         in_specs=[vmem] * 4 + [hbm] * 4,
-        out_specs=(vmem, vmem, hbm, hbm, hbm, hbm),
+        out_specs=(vmem, vmem, vmem),
         scratch_shapes=[
             V((2, C, 3 * C), BF), V((2, C, C), BF), V((2, C, FF), BF), V((2, FF, C), BF),
             dma((2, 4)),
@@ -300,9 +509,16 @@
             V((2, T, 3 * C), BF), V((2, HEADS, T, T), BF), V((2, T, C), BF),
             V((2, T, C), F32), V((2, T, C), BF), V((2, T, 128), F32),
             V((2, T, FF), F32), V((2, T, FF), BF), V((T, C), F32),
-            V((T, 3 * C), BF), V((T, C), BF), V((T, FF), BF), V((T, C), BF), V((T, C), BF),
-            V((2, 3 * C, C), BF), V((2, C, C), BF), V((2, FF, C), BF), V((2, C, FF), BF),
-            dma((2, 4)),
+            V((2, T, 3 * C), BF), V((2, T, C), BF), V((2, T, FF), BF), V((2, T, C), BF), V((T, C), BF),
+            V((2, T, C), BF), V((2, T, C), BF), V((2, T, C), BF), V((2, T, FF), BF),
+            V((2, 2, T, 384), BF), V((2, 2, T, 128), BF), V((2, 2, T, 512), BF), V((2, 2, T, 128), BF),
+            dma((2, 12)), dma((2, 12)),
+            V((2, 3, 4, 4, 64, C), BF), V((2, 3, 2, 2, 64, C), BF), V((2, 3, 2, 2, 64, C), BF),
+            V((2, 3, 2, 4, 64, C), BF),
+            V((2, 3, 4, 64, C), BF), V((2, 3, 2, 32, C), BF), V((2, 3, 2, 32, C), BF),
+            V((2, 3, 2, 64, C), BF),
+            V((2, 3, 4, 16, C), F32), V((2, 3, 3, 16, C), F32),
+            dma((2, 3, 15)), dma((2, 3, 15)),
         ],
         compiler_params=pltpu.CompilerParams(
             collective_id=0, has_side_effects=True, vmem_limit_bytes=60 * 2**20
@@ -317,17 +533,17 @@
     pieces = pieces.transpose(4, 3, 1, 5, 0, 2, 6).reshape(nlon * width, T)
     grid = lax.all_to_all(pieces, "lon", split_axis=0, concat_axis=0, tiled=True)
     up = upstream.reshape(levels * rows, WLON, C)
-    mixed, dgrid, *grads = layers(grid, up, w_qkv, w_proj, w_up, w_down)
+    mixed, dgrid, grads = layers(grid, up, w_qkv, w_proj, w_up, w_down)
     leaving = lax.all_to_all(dgrid, "lon", split_axis=0, concat_axis=0, tiled=True)
     leaving = leaving.reshape(nlon, width, 2, 2, levels, 3, 6).transpose(4, 2, 5, 1, 0, 3, 6)
-    shares = [
-        lax.psum_scatter(g, ("lat", "lon"), scatter_dimension=1, tiled=True).astype(F32)
-        for g in grads
-    ]
+    down = grads[:, 2].reshape(2, 4, 4, C).transpose(0, 1, 3, 2).reshape(2, FF, 4)
     return (
         mixed.reshape(upstream.shape),
         leaving.reshape(encoded.shape),
-        *[jnp.swapaxes(s, 1, 2) for s in shares],
+        jnp.swapaxes(grads[:, 0, 0:12], 1, 2),
+        jnp.swapaxes(grads[:, 0, 12:16], 1, 2),
+        jnp.swapaxes(grads[:, 1], 1, 2),
+        down,
     )
 
 

time: 904 us -> 137 us (0.15)
  the two profiles are of different devices: /device:TPU:0 before, /device:TPU:1 now
where the time goes in v2:
time: 137 us; the launch traced here: 135 us
  Pallas kernels  87.4 us (64%)
  local copies, waits for them, and re-layouts  17.4 us (13%)
  starting transfers between devices  16.5 us (12%)
  waiting for transfers between devices  12.8 us (9%)
    pallas_call x1, Pallas kernels, layers(): pl.pallas_call(layers_kernel, out_shape=(jax.ShapeDtypeStruct((12, WLON,...  87.4 us
    all_to_all x1, starting transfers between devices, on_device(): lax.all_to_all(pieces, 'lon', split_axis=0, concat_axis=0, tiled=True)  9.81 us
    unnamed x9, local copies, waits for them, and re-layouts  9.17 us
    all_to_all x1, waiting for transfers between devices, on_device(): lax.all_to_all(pieces, 'lon', split_axis=0, concat_axis=0, tiled=True)  7.35 us
    all_to_all x1, starting transfers between devices, on_device(): lax.all_to_all(dgrid, 'lon', split_axis=0, concat_axis=0, tiled=True)  6.73 us
    all_to_all x1, waiting for transfers between devices, on_device(): lax.all_to_all(dgrid, 'lon', split_axis=0, concat_axis=0, tiled=True)  5.45 us
  transfers between devices with their start and end apart: 2, of which 2 were waited for; matrix products, arithmetic and copies ran while one was open for 2% of the time, Pallas kernels for 0%

profile of v2, /device:TPU:1, one launch (start us, length us, event | category | flops | bytes accessed | tf_op | source)
XLA Modules:
  0.0 134.9 jit_solution(7564915589126003144)
XLA Ops:
  0.6 0.0 copy-start.1
  0.6 3.0 %copy.30 = bf16[2,6,16,384]{2,0,3,1:T(2,128)(2,1)S(1)} copy(bf16[2,6,16,384]{3,2,1,0:T(8,128)(2,1)} %param.8) | data formatting | bytes 294912 | tf_op args[0]
  3.6 0.9 copy.31
  4.6 1.4 %copy.32 = bf16[32,16,144]{2,1,0:T(8,128)(2,1)} copy(bf16[32,16,144]{0,1,2:T(8,128)(2,1)S(1)} %bitcast.31) | data formatting | bytes 294912 | tf_op jit(solution)/shard_map/all_to_all | solution.py:534
  6.0 9.8 %all-to-all-start = ((bf16[32,16,144]{2,1,0:T(8,128)(2,1)}), bf16[32,16,144]{2,1,0:T(8,128)(2,1)S(1)}, u32[]{:S(2)}, u32[]{:S(2)}) async-start(bf16[32,16,144]{2,1,0:T(8,128)(2,1)} %copy.32), calls=%async_computation | async-start | bytes 524288 | tf_op jit(solution)/shard_map/all_to_all | solution.py:534
  15.8 0.0 copy-done.1
  15.8 0.7 copy.33
  16.5 7.3 %all-to-all-done = bf16[32,16,144]{2,1,0:T(8,128)(2,1)S(1)} async-done(((bf16[32,16,144]{2,1,0:T(8,128)(2,1)}), bf16[32,16,144]{2,1,0:T(8,128)(2,1)S(1)}, u32[]{:S(2)}, u32[]{:S(2)}) %all-to-all-start) | async-done | bytes 147488 | tf_op jit(solution)/shard_map/all_to_all | solution.py:534
  23.9 0.0 copy-start
  23.9 0.7 copy-done
  24.6 87.4 %shard_map.127 = (bf16[12,12,512]{2,1,0:T(8,128)(2,1)}, bf16[512,144]{1,0:T(8,128)(2,1)}, f32[2,3,16,512]{3,2,1,0:T(8,128)}) custom-call(bf16[512,144]{1,0:T(8,128)(2,1)} %bitcast.33, bf16[12,12,512]{2,1,0:T(8,128)(2,1)} %bitcast.34, bf16[192,192]{1,0:T(8,128)(2,1)} %constant.4.clone.son_ref, bf16[144,192]{1,0:T(8,128)(2,1)} %constant.5.clone.tos_ref, ...), custom_call_target="tpu_custom_call" | custom-call | tf_op jit(solution)/shard_map/pallas_call | solution.py:494
  111.9 0.8 slice_bitcast_fusion.1
  112.8 1.5 %fusion = (f32[2,1,16,512]{3,2,1,0:T(8,128)S(1)}, f32[2,512,16]{1,2,0:T(8,128)}) fusion(f32[2,3,16,512]{3,2,1,0:T(8,128)} %get-tuple-element.11), kind=kLoop, calls=%fused_computation.3 | loop fusion | bytes 262144 | tf_op jit(solution)/shard_map/slice | solution.py:539
  114.3 1.7 %copy.37 = bf16[2,6,12,512]{3,0,2,1:T(2,128)(2,1)} copy(bf16[2,6,12,512]{3,2,1,0:T(8,128)(2,1)} %bitcast.36) | data formatting | bytes 294912
  116.0 6.7 %all-to-all-start.1 = ((bf16[32,16,144]{2,1,0:T(8,128)(2,1)}), bf16[32,16,144]{2,1,0:T(8,128)(2,1)S(1)}, u32[]{:S(2)}, u32[]{:S(2)}) async-start(bf16[32,16,144]{2,1,0:T(8,128)(2,1)} %bitcast.35), calls=%async_computation.1 | async-start | bytes 524288 | tf_op jit(solution)/shard_map/all_to_all | solution.py:537
  122.8 0.7 copy.39
  123.5 0.6 reshape_squeeze.3
  124.1 1.4 %slice_bitcast_fusion.2 = f32[2,512,4]{1,2,0:T(4,128)} fusion(f32[2,3,16,512]{3,2,1,0:T(8,128)} %get-tuple-element.11), kind=kLoop, calls=%fused_computation.2 | loop fusion | bytes 32768 | tf_op jit(solution)/shard_map/transpose | solution.py:544
  125.5 5.5 %all-to-all-done.1 = bf16[32,16,144]{2,1,0:T(8,128)(2,1)S(1)} async-done(((bf16[32,16,144]{2,1,0:T(8,128)(2,1)}), bf16[32,16,144]{2,1,0:T(8,128)(2,1)S(1)}, u32[]{:S(2)}, u32[]{:S(2)}) %all-to-all-start.1) | async-done | bytes 147488 | tf_op jit(solution)/shard_map/all_to_all | solution.py:537
  130.9 0.6 copy.34
  131.6 0.9 copy.35
  132.5 2.4 %copy.38 = bf16[2,6,16,384]{3,2,1,0:T(8,128)(2,1)} copy(bf16[2,6,16,384]{2,0,3,1:T(2,128)(2,1)S(1)} %bitcast.29) | data formatting | bytes 294912
Async XLA Ops:
  0.6 15.2 %copy-start.1 = (bf16[2,6,12,512]{3,0,2,1:T(2,128)(2,1)S(1)}, bf16[2,6,12,512]{3,0,2,1:T(2,128)(2,1)}, u32[]{:S(2)}) copy-start(bf16[2,6,12,512]{3,0,2,1:T(2,128)(2,1)} %param.9) | copy-start | bytes 442372
  6.0 17.9 %all-to-all-start = ((bf16[32,16,144]{2,1,0:T(8,128)(2,1)}), bf16[32,16,144]{2,1,0:T(8,128)(2,1)S(1)}, u32[]{:S(2)}, u32[]{:S(2)}) async-start(bf16[32,16,144]{2,1,0:T(8,128)(2,1)} %copy.32), calls=%async_computation | async-start | bytes 524288 | tf_op jit(solution)/shard_map/all_to_all | solution.py:534
  23.9 0.7 copy-start
  116.0 14.9 %all-to-all-start.1 = ((bf16[32,16,144]{2,1,0:T(8,128)(2,1)}), bf16[32,16,144]{2,1,0:T(8,128)(2,1)S(1)}, u32[]{:S(2)}, u32[]{:S(2)}) async-start(bf16[32,16,144]{2,1,0:T(8,128)(2,1)} %bitcast.35), calls=%async_computation.1 | async-start | bytes 524288 | tf_op jit(solution)/shard_map/all_to_all | solution.py:537

commit v3 on v2

--- a/solution.py
+++ b/solution.py
@@ -41,7 +41,13 @@
         slot = t // QUAD * SLOT + t % QUAD
         slots_of_natural[slot, (l * WLAT + r) * 16 + c] = 1
         tokens_of_slots[t, slot] = 1
-    return slots_of_natural, tokens_of_slots
+    tokens_of_natural = tokens_of_slots @ slots_of_natural
+    spread = np.zeros((32 * 16, 32 * WLON), np.float32)
+    for col in range(32 * WLON):
+        spread[col // WLON * 16 + col % WLON, col] = 1
+    swap = np.eye(1024, dtype=np.float32).reshape(8, 8, 16, 1024).swapaxes(0, 1).reshape(1024, 1024)
+    matrices = (slots_of_natural, tokens_of_slots, tokens_of_natural, spread, swap)
+    return [jnp.asarray(m, BF) for m in matrices]
 
 
 def nn(a, b):
@@ -69,10 +75,11 @@
 
 
 def layers_kernel(
-    grid_ref, up_ref, son_ref, tos_ref, wqkv_hbm, wproj_hbm, wup_hbm, wdown_hbm,
-    mixed_ref, dgrid_ref, grads_ref,
+    enc_ref, up_ref, son_ref, tos_ref, ton_ref, spread_ref, swap_hbm,
+    wqkv_hbm, wproj_hbm, wup_hbm, wdown_hbm,
+    mixed_ref, denc_ref, oqkv_ref, oproj_ref, oup_ref, odown_ref,
     wqkv, wproj, wup, wdown, wsem,
-    nat, send, recv, send_sem, recv_sem,
+    swap, swap_sem, leave, came, leave2, came2, lane_send, lane_recv, own_sem, nat2, turned, nat, send, recv, send_sem, recv_sem,
     xs, n1h, n1, r1, us, ps, att, n2h, n2, r2, gp, hs, acc, eq, ep, eu, ed, dab,
     pn1, patt, pn2, phs, peq, pep, peu, ped, pair_send, pair_recv,
     part, fwd, fsum, side, part2, fwd2, fsum2, side2, part3, side3, ring_send, ring_recv,
@@ -94,6 +101,8 @@
     partner = (i + 1 - 2 * core, j)
 
     weights = ((wqkv_hbm, wqkv), (wproj_hbm, wproj), (wup_hbm, wup), (wdown_hbm, wdown))
+    swap_fetch = pltpu.make_async_copy(swap_hbm, swap, swap_sem)
+    swap_fetch.start()
     fetches = []
     for k in range(2):
         for w, (src, dst) in enumerate(weights):
@@ -107,7 +116,50 @@
     greeted += [along(axis, steps) for axis in "xyz" for steps in (1, 2, 3)] + [partner]
     for other in greeted:
         pl.semaphore_signal(barrier, inc=1, device_id=other, device_id_type=MESH)
-    pl.semaphore_wait(barrier, len(greeted))
+
+    @pl.loop(1, nlon)
+    def _(step):
+        pl.semaphore_signal(barrier, inc=1, device_id=device(0, step), device_id_type=MESH)
+
+    columns_first = nt(spread_ref[...], enc_ref[...].reshape(12 * 16, 32 * WLON)).astype(BF)
+    leave[:, 0] = columns_first[:, 0:128].reshape(32, 16, 128)
+    leave[:, 1, :, 0:64] = columns_first[:, 128:192].reshape(32, 16, 64)
+    leave[:, 1, :, 64:128] = jnp.zeros((32, 16, 64), BF)
+    pl.semaphore_wait(barrier, len(greeted) + nlon - 1)
+    mine = pl.ds(pl.multiple_of(lax.rem(j, 8) * 128, 128), 128)
+
+    def lane_copy(step, event):
+        to = lax.rem(j + step, nlon)
+        if event == 0:
+            src, dst = leave.at[to], came.at[:, j // 8, :, mine]
+        else:
+            src, dst = leave2.at[to], came2.at[j]
+        return pltpu.make_async_remote_copy(
+            src_ref=src, dst_ref=dst, send_sem=lane_send.at[event, step], recv_sem=lane_recv.at[event, step],
+            device_id=(i, to), device_id_type=MESH,
+        )
+
+    def lane_start(event):
+        @pl.loop(1, nlon)
+        def _(step):
+            lane_copy(step, event).start()
+
+        if event == 0:
+            src, dst = leave.at[j], came.at[:, j // 8, :, mine]
+        else:
+            src, dst = leave2.at[j], came2.at[j]
+        own = pltpu.make_async_copy(src, dst, own_sem.at[event])
+        own.start()
+        return own
+
+    def lane_finish(event, own):
+        own.wait()
+
+        @pl.loop(1, nlon)
+        def _(step):
+            lane_copy(step, event).wait()
+
+    own = lane_start(0)
 
     def remote(src, dst, sems, index, to):
         copy = pltpu.make_async_remote_copy(
@@ -229,7 +281,15 @@
         t = {"x": x, "y": y, "z": z}[orders[p][2]]
         for copy in rings[k, p, 2]:
             copy.wait_recv()
-        grads_ref[k, p] = part3[k, p, t] + side3[k, p, 0] + side3[k, p, 1] + side3[k, p, 2]
+        total = part3[k, p, t] + side3[k, p, 0] + side3[k, p, 1] + side3[k, p, 2]
+        if p == 0:
+            oqkv_ref[:, k, :] = total[0:12]
+            oproj_ref[k] = total[12:16]
+        elif p == 1:
+            oup_ref[k] = total
+        else:
+            for hb in range(4):
+                odown_ref[k, :, hb * C : hb * C + C] = total[4 * hb : 4 * hb + 4]
 
     def both(k, name, hi, own, theirs):
         src, dst = cut[name]
@@ -421,7 +481,15 @@
     def nothing():
         pass
 
-    first = forward(0, jnp.transpose(grid_ref[...].astype(F32)))
+    swap_fetch.wait()
+    lane_finish(0, own)
+    for half in range(2):
+        moved = nn(came[half].reshape(64, 1024), swap[...]).astype(BF)
+        for lr in range(8 if half == 0 else 4):
+            for g in range(4):
+                at = (slice(128 * half + 16 * lr, 128 * half + 16 * lr + 16), slice(128 * g, 128 * g + 128))
+                nat2[at] = moved[16 * g : 16 * g + 16, 128 * lr : 128 * lr + 128]
+    first = forward(0, nn(ton_ref[...], nat2[...]))
     put(1, first.astype(BF))
     finish(exchange(1, True))
     second = forward(1, got(1))
@@ -465,7 +533,23 @@
     ring_end(0, 2, 0)
     ring_end(0, 1, 0)
     d_first = backward_end(0)
-    dgrid_ref[...] = jnp.transpose(d_first).astype(BF)
+    nat2[...] = tn(ton_ref[...], d_first.astype(BF)).astype(BF)
+    for half in range(2):
+        for lr in range(8):
+            for g in range(4):
+                at = (slice(16 * g, 16 * g + 16), slice(128 * lr, 128 * lr + 128))
+                if half == 1 and lr >= 4:
+                    turned[half, at[0], at[1]] = jnp.zeros((16, 128), BF)
+                else:
+                    row = 128 * half + 16 * lr
+                    turned[half, at[0], at[1]] = nat2[row : row + 16, 128 * g : 128 * g + 128]
+        moved = nn(turned[half], swap[...]).astype(BF)
+        for g in range(4):
+            for lane_block in range(8):
+                leave2[8 * g + lane_block, half] = moved[
+                    16 * g : 16 * g + 16, 128 * lane_block : 128 * lane_block + 128
+                ]
+    own = lane_start(1)
     ring_mid(0, 0, 0)
     ring_mid(0, 2, 1)
     ring_mid(0, 1, 1)
@@ -479,14 +563,18 @@
     ring_mid(0, 0, 1)
     ring_last(0, 2)
     ring_last(0, 1)
+    lane_finish(1, own)
+    for half in range(2):
+        rows = tn(came2[:, half].reshape(512, 128), spread_ref[...]).astype(BF)
+        n = 8 if half == 0 else 4
+        denc_ref[8 * half : 8 * half + n] = rows[0 : 16 * n].reshape(n, 16, 32 * WLON)
     ring_end(0, 0, 1)
     ring_last(0, 0)
     for copy in sent:
         copy.wait_send()
 
 
-def layers(grid, upstream, w_qkv, w_proj, w_up, w_down):
-    son, tos = permutations()
+def layers(encoded, upstream, w_qkv, w_proj, w_up, w_down):
     vmem = pl.BlockSpec(memory_space=pltpu.VMEM)
     hbm = pl.BlockSpec(memory_space=pl.ANY)
     dma = pltpu.SemaphoreType.DMA
@@ -495,14 +583,20 @@
         layers_kernel,
         out_shape=(
             jax.ShapeDtypeStruct((12, WLON, C), BF),
-            jax.ShapeDtypeStruct((C, T), BF),
-            jax.ShapeDtypeStruct((2, 3, 16, C), F32),
+            jax.ShapeDtypeStruct((12, 16, 32 * WLON), BF),
+            jax.ShapeDtypeStruct((12, 2, C), F32),
+            jax.ShapeDtypeStruct((2, 4, C), F32),
+            jax.ShapeDtypeStruct((2, 16, C), F32),
+            jax.ShapeDtypeStruct((2, 4, FF), F32),
         ),
-        in_specs=[vmem] * 4 + [hbm] * 4,
-        out_specs=(vmem, vmem, vmem),
+        in_specs=[vmem] * 6 + [hbm] * 5,
+        out_specs=(vmem,) * 6,
         scratch_shapes=[
             V((2, C, 3 * C), BF), V((2, C, C), BF), V((2, C, FF), BF), V((2, FF, C), BF),
             dma((2, 4)),
+            V((1024, 1024), BF), dma, V((32, 2, 16, 128), BF), V((2, 4, 16, 1024), BF),
+            V((32, 2, 16, 128), BF), V((32, 2, 16, 128), BF), dma((2, 32)), dma((2, 32)), dma((2,)),
+            V((12 * 16, C), BF), V((2, 64, 1024), BF),
             V((12, 16, C), BF), V((4, 4, SLOT, C), BF), V((4, 4, SLOT, C), BF),
             dma((4, 4)), dma((4, 4)),
             V((2, T, C), F32), V((2, T, C), F32), V((2, T, C), BF), V((2, T, 128), F32),
@@ -523,27 +617,20 @@
         compiler_params=pltpu.CompilerParams(
             collective_id=0, has_side_effects=True, vmem_limit_bytes=60 * 2**20
         ),
-    )(grid, upstream, jnp.asarray(son, BF), jnp.asarray(tos, BF), w_qkv, w_proj, w_up, w_down)
+    )(encoded, upstream, *permutations(), w_qkv, w_proj, w_up, w_down)
 
 
 def on_device(encoded, upstream, w_qkv, w_proj, w_up, w_down):
-    levels, rows, width, cols = encoded.shape
-    nlon = cols // WLON
-    pieces = encoded.reshape(levels, 2, 3, width, nlon, 2, 6)
-    pieces = pieces.transpose(4, 3, 1, 5, 0, 2, 6).reshape(nlon * width, T)
-    grid = lax.all_to_all(pieces, "lon", split_axis=0, concat_axis=0, tiled=True)
-    up = upstream.reshape(levels * rows, WLON, C)
-    mixed, dgrid, grads = layers(grid, up, w_qkv, w_proj, w_up, w_down)
-    leaving = lax.all_to_all(dgrid, "lon", split_axis=0, concat_axis=0, tiled=True)
-    leaving = leaving.reshape(nlon, width, 2, 2, levels, 3, 6).transpose(4, 2, 5, 1, 0, 3, 6)
-    down = grads[:, 2].reshape(2, 4, 4, C).transpose(0, 1, 3, 2).reshape(2, FF, 4)
+    mixed, dencoded, qkv, proj, up, down = layers(
+        encoded.reshape(12, 16, 32 * WLON), upstream.reshape(12, WLON, C), w_qkv, w_proj, w_up, w_down
+    )
     return (
         mixed.reshape(upstream.shape),
-        leaving.reshape(encoded.shape),
-        jnp.swapaxes(grads[:, 0, 0:12], 1, 2),
-        jnp.swapaxes(grads[:, 0, 12:16], 1, 2),
-        jnp.swapaxes(grads[:, 1], 1, 2),
-        down,
+        dencoded.reshape(encoded.shape),
+        qkv.transpose(1, 2, 0),
+        proj.swapaxes(1, 2),
+        up.swapaxes(1, 2),
+        down.swapaxes(1, 2),
     )
 
 

time: 137 us -> 114 us (0.83); the launches traced: 135 us -> 114 us
  starting transfers between devices: 16.5 us -> 0 us
  Pallas kernels: 87.4 us -> 102 us
  waiting for transfers between devices: 12.8 us -> 0 us
  local copies, waits for them, and re-layouts: 17.4 us -> 10.6 us
    all_to_all x2 -> x0, starting transfers between devices: 16.5 us -> none  [the longest x1 9.81 us: on_device(): lax.all_to_all(pieces, 'lon', split_axis=0, concat_axis=0, tiled=True)]
    pallas_call x1, Pallas kernels: 87.4 us -> 102 us  [layers(): pl.pallas_call(layers_kernel, out_shape=(jax.ShapeDtypeStruct((12, WLON,...]
    all_to_all x2 -> x0, waiting for transfers between devices: 12.8 us -> none  [the longest x1 7.35 us: on_device(): lax.all_to_all(pieces, 'lon', split_axis=0, concat_axis=0, tiled=True)]
    transpose x4 -> x0, local copies, waits for them, and re-layouts: 4.05 us -> none  [the longest x1 1.37 us: on_device(): jnp.swapaxes(grads[:, 0, 12:16], 1, 2)]
    all_to_all x2 -> x0, local copies, waits for them, and re-layouts: 2.05 us -> none  [the longest x1 1.4 us: on_device(): lax.all_to_all(pieces, 'lon', split_axis=0, concat_axis=0, tiled=True)]
    slice x1 -> x0, local copies, waits for them, and re-layouts: 1.51 us -> none  [on_device(): grads[:, 2].reshape(2, 4, 4, C).transpose(0, 1, 3, 2).reshape(2, FF, 4)]
    unnamed x9 -> x7, local copies, waits for them, and re-layouts: 9.17 us -> 10.6 us
  transfers between devices with their start and end apart: 2 -> 0, of which waited for: 2 -> 0; matrix products, arithmetic and copies ran while one was open for 2% -> 0% of each run, Pallas kernels for 0% -> 0%
where the time goes in v3:
time: 114 us
  Pallas kernels  102 us (89%)
  local copies, waits for them, and re-layouts  10.6 us (9%)
    pallas_call x1, Pallas kernels, layers(): pl.pallas_call(layers_kernel, out_shape=(jax.ShapeDtypeStruct((12, WLON,...  102 us
    unnamed x7, local copies, waits for them, and re-layouts  10.6 us

profile of v3, /device:TPU:1, one launch (start us, length us, event | category | flops | bytes accessed | tf_op | source)
XLA Modules:
  0.0 113.6 jit_solution(10185350654490389032)
XLA Ops:
  0.6 1.6 %copy.17 = bf16[2,6,12,512]{3,2,1,0:T(8,128)(2,1)} copy(bf16[2,6,12,512]{3,0,2,1:T(2,128)(2,1)} %param.12) | data formatting | bytes 294912 | tf_op args[1]
  2.2 102.3 %shard_map.154 = (bf16[12,12,512]{2,1,0:T(8,128)(2,1)}, bf16[12,16,384]{2,1,0:T(8,128)(2,1)}, f32[12,2,512]{2,1,0:T(2,128)}, f32[2,4,512]{2,1,0:T(4,128)}, f32[2,16,512]{2,1,0:T(8,128)}, /*index=5*/f32[2,4,2048]{2,1,0:T(4,128)}) custom-call(bf16[12,16,384]{2,1,0:T(8,128)(2,1)} %bitcast.11, bf16[12,12,512]{2,1,0:T(8,128)(2,1)} %bitcast.8, ...), custom_call_target="tpu_custom_call" | custom-call | tf_op jit(solution)/shard_map/pallas_call | solution.py:582
  104.6 1.7 %copy.18 = bf16[2,6,12,512]{3,0,2,1:T(2,128)(2,1)} copy(bf16[2,6,12,512]{3,2,1,0:T(8,128)(2,1)} %bitcast.9) | data formatting | bytes 294912
  106.3 1.6 %copy.24 = bf16[2,6,16,384]{3,2,1,0:T(8,128)(2,1)} copy(bf16[2,6,16,384]{3,2,1,0:T(8,128)(2,1)} %bitcast.10) | data formatting | bytes 294912
  107.9 1.4 %copy.25 = f32[2,512,12]{1,0,2:T(2,128)} copy(f32[2,512,12]{1,0,2:T(2,128)} %bitcast.14) | data formatting | bytes 98304
  109.3 1.3 %copy.26 = f32[2,512,4]{1,2,0:T(4,128)} copy(f32[2,512,4]{1,2,0:T(4,128)} %bitcast.15) | data formatting | bytes 32768
  110.7 1.5 %copy.27 = f32[2,512,16]{1,2,0:T(8,128)} copy(f32[2,512,16]{1,2,0:T(8,128)} %bitcast.13) | data formatting | bytes 131072
  112.1 1.5 %copy.28 = f32[2,2048,4]{1,2,0:T(4,128)} copy(f32[2,2048,4]{1,2,0:T(4,128)} %bitcast.12) | data formatting | bytes 131072

commit v4 on v3

--- a/solution.py
+++ b/solution.py
@@ -35,18 +35,19 @@
 
 
 def permutations():
-    slots_of_natural = np.zeros((4 * SLOT, 12 * 16), np.float32)
+    slots_of_natural = np.zeros((4 * SLOT, T), np.float32)
     tokens_of_slots = np.zeros((T, 4 * SLOT), np.float32)
+    tokens_of_padded = np.zeros((T, 12 * 16), np.float32)
     for t, (l, r, c) in enumerate(quadrant_order()):
         slot = t // QUAD * SLOT + t % QUAD
-        slots_of_natural[slot, (l * WLAT + r) * 16 + c] = 1
+        slots_of_natural[slot, (r * WLON + c) * LEV + l] = 1
         tokens_of_slots[t, slot] = 1
-    tokens_of_natural = tokens_of_slots @ slots_of_natural
+        tokens_of_padded[t, (l * WLAT + r) * 16 + c] = 1
     spread = np.zeros((32 * 16, 32 * WLON), np.float32)
     for col in range(32 * WLON):
         spread[col // WLON * 16 + col % WLON, col] = 1
     swap = np.eye(1024, dtype=np.float32).reshape(8, 8, 16, 1024).swapaxes(0, 1).reshape(1024, 1024)
-    matrices = (slots_of_natural, tokens_of_slots, tokens_of_natural, spread, swap)
+    matrices = (slots_of_natural, tokens_of_slots, tokens_of_padded, spread, swap)
     return [jnp.asarray(m, BF) for m in matrices]
 
 
@@ -75,14 +76,16 @@
 
 
 def layers_kernel(
-    enc_ref, up_ref, son_ref, tos_ref, ton_ref, spread_ref, swap_hbm,
+    enc_hbm, up_hbm, son_hbm, tos_hbm, ton_hbm, spread_hbm, swap_hbm,
     wqkv_hbm, wproj_hbm, wup_hbm, wdown_hbm,
-    mixed_ref, denc_ref, oqkv_ref, oproj_ref, oup_ref, odown_ref,
+    mixed_hbm, denc_hbm, oqkv_hbm, oproj_hbm, oup_hbm, odown_hbm,
+    enc_ref, up_ref, son_ref, tos_ref, ton_ref, spread_ref, in_sem,
+    mixed_ref, denc_ref, oqkv_ref, oproj_ref, oup_ref, odown_ref, out_sem,
     wqkv, wproj, wup, wdown, wsem,
-    swap, swap_sem, leave, came, leave2, came2, lane_send, lane_recv, own_sem, nat2, turned, nat, send, recv, send_sem, recv_sem,
+    swap, leave, came, leave2, came2, lane_send, lane_recv, own_sem, nat2, turned, send, recv, send_sem, recv_sem,
     xs, n1h, n1, r1, us, ps, att, n2h, n2, r2, gp, hs, acc, eq, ep, eu, ed, dab,
     pn1, patt, pn2, phs, peq, pep, peu, ped, pair_send, pair_recv,
-    part, fwd, fsum, side, part2, fwd2, fsum2, side2, part3, side3, ring_send, ring_recv,
+    part, fwd, fsum, side, plane_out, plane_in, ring_send, ring_recv, plane_send, plane_recv,
 ):
     i, j = lax.axis_index("lat"), lax.axis_index("lon")
     nlat, nlon = lax.axis_size("lat"), lax.axis_size("lon")
@@ -98,11 +101,25 @@
         at[axis] = lax.rem(at[axis] + steps + 4, 4)
         return (at["x"] // 2 * 2 + core, at["y"] * 8 + lax.rem(at["x"], 2) * 4 + at["z"])
 
+    def beside(axis, steps, other, others):
+        at = {"x": x, "y": y, "z": z}
+        at[axis] = lax.rem(at[axis] + steps + 4, 4)
+        at[other] = lax.rem(at[other] + others + 4, 4)
+        return (at["x"] // 2 * 2 + core, at["y"] * 8 + lax.rem(at["x"], 2) * 4 + at["z"])
+
     partner = (i + 1 - 2 * core, j)
 
     weights = ((wqkv_hbm, wqkv), (wproj_hbm, wproj), (wup_hbm, wup), (wdown_hbm, wdown))
-    swap_fetch = pltpu.make_async_copy(swap_hbm, swap, swap_sem)
-    swap_fetch.start()
+    inputs = {}
+    for at, (name, src, dst) in enumerate(
+        (
+            ("enc", enc_hbm, enc_ref), ("spread", spread_hbm, spread_ref), ("up", up_hbm, up_ref),
+            ("son", son_hbm, son_ref), ("tos", tos_hbm, tos_ref), ("ton", ton_hbm, ton_ref),
+            ("swap", swap_hbm, swap),
+        )
+    ):
+        inputs[name] = pltpu.make_async_copy(src, dst, in_sem.at[at])
+        inputs[name].start()
     fetches = []
     for k in range(2):
         for w, (src, dst) in enumerate(weights):
@@ -114,6 +131,7 @@
     offsets = ((0, 1), (1, 0), (1, 1), (0, -1), (-1, 0), (-1, -1))
     greeted = [device(di, dj) for di, dj in offsets]
     greeted += [along(axis, steps) for axis in "xyz" for steps in (1, 2, 3)] + [partner]
+    greeted += [beside("x", dx, other, d) for other in "yz" for dx in (1, 2, 3) for d in (1, 2, 3)]
     for other in greeted:
         pl.semaphore_signal(barrier, inc=1, device_id=other, device_id_type=MESH)
 
@@ -121,6 +139,8 @@
     def _(step):
         pl.semaphore_signal(barrier, inc=1, device_id=device(0, step), device_id_type=MESH)
 
+    inputs["enc"].wait()
+    inputs["spread"].wait()
     columns_first = nt(spread_ref[...], enc_ref[...].reshape(12 * 16, 32 * WLON)).astype(BF)
     leave[:, 0] = columns_first[:, 0:128].reshape(32, 16, 128)
     leave[:, 1, :, 0:64] = columns_first[:, 128:192].reshape(32, 16, 64)
@@ -198,102 +218,99 @@
         for copy in pairs[k, name]:
             copy.wait_recv()
 
-    orders = ("xyz", "zyx", "yxz")
+    orders = ("xyz", "yxz", "zyx", "zyx", "xyz", "yxz")
+    where = {"x": x, "y": y, "z": z}
     rings = {}
 
-    def chunk(k, p, phase, t, half):
-        t = lax.rem(t + 4, 4)
-        if phase == 0:
-            return part.at[k, p, t, pl.ds(2 * half, 2)]
-        return part2.at[k, p, t, pl.ds(32 * half, 32)]
-
-    def ring_bufs(k, p, phase):
-        if phase == 0:
-            halves = [[side.at[k, p, s, pl.ds(2 * h, 2)] for h in range(2)] for s in range(2)]
-            return [fwd.at[k, p, s] for s in range(2)], [fsum.at[k, p, s] for s in range(2)], halves
-        halves = [[side2.at[k, p, s, pl.ds(32 * h, 32)] for h in range(2)] for s in range(2)]
-        return [fwd2.at[k, p, s] for s in range(2)], [fsum2.at[k, p, s] for s in range(2)], halves
+    def chunk(k, p, t, half):
+        return part.at[k, p, lax.rem(t + 4, 4), pl.ds(2 * half, 2)]
 
     def f32(ref):
         return ref[...].astype(F32)
 
-    def ring_start(k, p, phase):
-        axis = orders[p][phase]
-        t = {"x": x, "y": y, "z": z}[axis]
+    def ring_start(k, p):
+        axis = orders[p][0]
+        t = where[axis]
         after, before = along(axis, 1), along(axis, -1)
-        f, _, halves = ring_bufs(k, p, phase)
         sems = (ring_send, ring_recv)
-        o = 6 * phase
-        rings[k, p, phase] = [
-            remote(chunk(k, p, phase, t + 2, 0), f[0], sems, (k, p, o), after),
-            remote(chunk(k, p, phase, t + 2, 1), f[1], sems, (k, p, o + 1), before),
-            remote(chunk(k, p, phase, t + 1, 1), halves[0][1], sems, (k, p, o + 2), after),
-            remote(chunk(k, p, phase, t - 1, 0), halves[1][0], sems, (k, p, o + 3), before),
+        rings[k, p] = [
+            remote(chunk(k, p, t + 2, 0), fwd.at[k, p, 0], sems, (k, p, 0), after),
+            remote(chunk(k, p, t + 2, 1), fwd.at[k, p, 1], sems, (k, p, 1), before),
+            remote(chunk(k, p, t + 1, 1), side.at[k, p, 0, pl.ds(2, 2)], sems, (k, p, 2), after),
+            remote(chunk(k, p, t - 1, 0), side.at[k, p, 1, pl.ds(0, 2)], sems, (k, p, 3), before),
         ]
 
-    def ring_mid(k, p, phase):
-        axis = orders[p][phase]
-        t = {"x": x, "y": y, "z": z}[axis]
+    def ring_mid(k, p):
+        axis = orders[p][0]
+        t = where[axis]
         after, before = along(axis, 1), along(axis, -1)
-        f, fs, halves = ring_bufs(k, p, phase)
-        copies = rings[k, p, phase]
+        copies = rings[k, p]
         sems = (ring_send, ring_recv)
-        o = 6 * phase
         copies[0].wait_recv()
-        fs[0][...] = (f32(f[0]) + f32(chunk(k, p, phase, t + 1, 0))).astype(BF)
-        copies.append(remote(fs[0], halves[0][0], sems, (k, p, o + 4), after))
+        fsum[k, p, 0] = (f32(fwd.at[k, p, 0]) + f32(chunk(k, p, t + 1, 0))).astype(BF)
+        copies.append(remote(fsum.at[k, p, 0], side.at[k, p, 0, pl.ds(0, 2)], sems, (k, p, 4), after))
         copies[1].wait_recv()
-        fs[1][...] = (f32(f[1]) + f32(chunk(k, p, phase, t - 1, 1))).astype(BF)
-        copies.append(remote(fs[1], halves[1][1], sems, (k, p, o + 5), before))
-
-    def ring_end(k, p, phase):
-        axis = orders[p][phase]
-        t = {"x": x, "y": y, "z": z}[axis]
-        for copy in rings[k, p, phase][2:]:
+        fsum[k, p, 1] = (f32(fwd.at[k, p, 1]) + f32(chunk(k, p, t - 1, 1))).astype(BF)
+        copies.append(remote(fsum.at[k, p, 1], side.at[k, p, 1, pl.ds(2, 2)], sems, (k, p, 5), before))
+
+    def plane_copy(k, p, step):
+        _, second, third = orders[p]
+        d2, d3 = step // 4, lax.rem(step, 4)
+        src = plane_out.at[k, p, lax.rem(where[second] + d2, 4), lax.rem(where[third] + d3, 4)]
+        return pltpu.make_async_remote_copy(
+            src_ref=src, dst_ref=plane_in.at[k, p, step], send_sem=plane_send.at[k, p, step],
+            recv_sem=plane_recv.at[k, p, step], device_id=beside(second, d2, third, d3), device_id_type=MESH,
+        )
+
+    def ring_end(k, p):
+        for copy in rings[k, p][2:]:
             copy.wait_recv()
-        if phase == 0:
-            total = f32(part.at[k, p, t]) + f32(side.at[k, p, 0]) + f32(side.at[k, p, 1])
-            part2[k, p] = total.astype(BF)
-            ring_start(k, p, 1)
-            return
-        total = f32(part2.at[k, p, t]) + f32(side2.at[k, p, 0]) + f32(side2.at[k, p, 1])
-        for s in range(4):
-            if p == 0:
-                rows = (total[12 * s : 12 * s + 12], total[48 + 4 * s : 52 + 4 * s])
-                rows = jnp.concatenate(rows, 0)
-            elif p == 1:
-                rows = total[16 * s : 16 * s + 16]
-            else:
-                rows = [total[16 * hb + 4 * s : 16 * hb + 4 * s + 4] for hb in range(4)]
-                rows = jnp.concatenate(rows, 0)
-            part3[k, p, s] = rows
-        axis = orders[p][2]
-        t = {"x": x, "y": y, "z": z}[axis]
-        rings[k, p, 2] = [
-            remote(
-                part3.at[k, p, lax.rem(t + s, 4)], side3.at[k, p, s - 1], (ring_send, ring_recv),
-                (k, p, 11 + s), along(axis, s),
-            )
-            for s in (1, 2, 3)
-        ]
+        t = where[orders[p][0]]
+        total = f32(part.at[k, p, t]) + f32(side.at[k, p, 0]) + f32(side.at[k, p, 1])
+        for s2 in range(4):
+            for s3 in range(4):
+                if p // 2 == 0:
+                    rows = (total[s2, 12 * s3 : 12 * s3 + 12], total[s2, 48 + 4 * s3 : 52 + 4 * s3])
+                    rows = jnp.concatenate(rows, 0)
+                elif p // 2 == 1:
+                    rows = total[s2, 16 * s3 : 16 * s3 + 16]
+                else:
+                    rows = [total[s2, 16 * hb + 4 * s3 : 16 * hb + 4 * s3 + 4] for hb in range(4)]
+                    rows = jnp.concatenate(rows, 0)
+                plane_out[k, p, s2, s3] = rows.astype(BF)
+
+        @pl.loop(1, 16)
+        def _(step):
+            plane_copy(k, p, step).start()
 
     def ring_last(k, p):
-        t = {"x": x, "y": y, "z": z}[orders[p][2]]
-        for copy in rings[k, p, 2]:
-            copy.wait_recv()
-        total = part3[k, p, t] + side3[k, p, 0] + side3[k, p, 1] + side3[k, p, 2]
-        if p == 0:
-            oqkv_ref[:, k, :] = total[0:12]
-            oproj_ref[k] = total[12:16]
-        elif p == 1:
-            oup_ref[k] = total
+        @pl.loop(1, 16)
+        def _(step):
+            plane_copy(k, p, step).wait()
+
+        _, second, third = orders[p]
+        total = f32(plane_out.at[k, p, where[second], where[third]])
+        for step in range(1, 16):
+            total += f32(plane_in.at[k, p, step])
+        lanes = slice(256 * (p % 2), 256 * (p % 2) + 256)
+        if p // 2 == 0:
+            oqkv_ref[:, k, lanes] = total[0:12]
+            oproj_ref[k, :, lanes] = total[12:16]
+        elif p // 2 == 1:
+            oup_ref[k, :, lanes] = total
         else:
             for hb in range(4):
-                odown_ref[k, :, hb * C : hb * C + C] = total[4 * hb : 4 * hb + 4]
+                at = slice(hb * C + lanes.start, hb * C + lanes.stop)
+                odown_ref[k, :, at] = total[4 * hb : 4 * hb + 4]
 
     def both(k, name, hi, own, theirs):
         src, dst = cut[name]
         return tn(src[k, :, columns(name, hi, core)], own) + tn(dst[k, hi], theirs)
+
+    def keep(k, p, first, second, rows, g):
+        for s in range(2):
+            at = (first, second) if orders[p + s][0] == orders[p][0] else (second, first)
+            part[k, p + s, at[0], at[1], rows, :] = g[:, 256 * s : 256 * s + 256]
 
     def grads_a(k):
         for name in ("n1", "att", "ep", "eq"):
@@ -301,11 +318,12 @@
         for hi in range(2):
             g = both(k, "eq", hi, n1[k], pn1[k]).astype(BF)
             for at in range(8):
-                part[k, 0, 2 * hi + at % 2, at // 2, 0:48, :] = g[48 * at : 48 * at + 48]
+                keep(k, 0, 2 * hi + at % 2, at // 2, slice(0, 48), g[48 * at : 48 * at + 48])
             g = both(k, "ep", hi, att[k], patt[k]).astype(BF)
             for at in range(8):
-                part[k, 0, 2 * hi + at % 2, at // 2, 48:64, :] = g[16 * at : 16 * at + 16]
-        ring_start(k, 0, 0)
+                keep(k, 0, 2 * hi + at % 2, at // 2, slice(48, 64), g[16 * at : 16 * at + 16])
+        ring_start(k, 0)
+        ring_start(k, 1)
 
     def grads_b(k):
         for name in ("n2", "eu"):
@@ -314,8 +332,9 @@
             g = both(k, "eu", hi, n2[k], pn2[k]).astype(BF)
             for at in range(32):
                 row = (2 * hi + at // 4 % 2) * 16
-                part[k, 1, at % 4, at // 8, row : row + 16, :] = g[16 * at : 16 * at + 16]
-        ring_start(k, 1, 0)
+                keep(k, 2, at % 4, at // 8, slice(row, row + 16), g[16 * at : 16 * at + 16])
+        ring_start(k, 2)
+        ring_start(k, 3)
 
     def grads_c(k):
         for name in ("hs", "ed"):
@@ -326,8 +345,9 @@
                 g = both(k, "ed", hi, hs[k, :, cols], phs[k, :, cols]).astype(BF)
                 for at in range(8):
                     row = 16 * hb
-                    part[k, 2, at // 2, 2 * hi + at % 2, row : row + 16, :] = g[16 * at : 16 * at + 16]
-        ring_start(k, 2, 0)
+                    keep(k, 4, 2 * hi + at % 2, at // 2, slice(row, row + 16), g[16 * at : 16 * at + 16])
+        ring_start(k, 4)
+        ring_start(k, 5)
 
     def exchange(event, forward):
         copies = []
@@ -356,9 +376,9 @@
     def got(event):
         return nn(tos_ref[...], recv[event].reshape(4 * SLOT, C))
 
-    nat[...] = jnp.zeros_like(nat)
-    nat[:, 0:WLON, :] = up_ref[...]
-    send[0] = nn(son_ref[...], nat[...].reshape(12 * 16, C)).astype(BF).reshape(4, SLOT, C)
+    for name in ("up", "son", "tos", "ton"):
+        inputs[name].wait()
+    send[0] = nn(son_ref[...], up_ref[...].reshape(T, C)).astype(BF).reshape(4, SLOT, C)
     up_copies = exchange(0, True)
 
     lane = lax.broadcasted_iota(jnp.int32, (1, 128), 1)
@@ -469,9 +489,9 @@
             eq[k, :, at(1)] = dk.astype(BF)
             eq[k, :, at(2)] = dv.astype(BF)
 
-        pl.loop(0, 2)(heads)
-        amid()
-        pl.loop(2, 4)(heads)
+        for half in range(2):
+            pl.loop(2 * half, 2 * half + 2)(heads)
+            amid(half)
         give(k, "eq")
 
     def backward_end(k):
@@ -481,7 +501,7 @@
     def nothing():
         pass
 
-    swap_fetch.wait()
+    inputs["swap"].wait()
     lane_finish(0, own)
     for half in range(2):
         moved = nn(came[half].reshape(64, 1024), swap[...]).astype(BF)
@@ -497,41 +517,46 @@
     mixed_copies = exchange(2, False)
     finish(up_copies)
 
-    def amid_one():
-        ring_mid(1, 2, 0)
+    def mids(k, parts):
+        for p in parts:
+            ring_mid(k, p)
+
+    def ends(k, parts):
+        for p in parts:
+            ring_end(k, p)
+
+    def lasts(k, parts):
+        for p in parts:
+            ring_last(k, p)
+
+    def amid_one(half):
+        if half == 1:
+            mids(1, (4, 5))
 
     backward(1, got(0), nothing, nothing, amid_one)
-    ring_mid(1, 1, 0)
     d_second = backward_end(1)
     put(3, d_second.astype(BF))
     mid_copies = exchange(3, False)
-    ring_end(1, 2, 0)
     grads_a(1)
-    ring_end(1, 1, 0)
-    ring_mid(1, 2, 1)
+    mids(1, (2, 3))
     finish(mid_copies)
 
     def up_zero():
-        ring_mid(1, 0, 0)
-        ring_mid(1, 1, 1)
-        ring_end(1, 2, 1)
+        ends(1, (4, 5))
+        mids(1, (0, 1))
 
     def proj_zero():
-        ring_end(1, 0, 0)
-        ring_end(1, 1, 1)
-        ring_last(1, 2)
-
-    def amid_zero():
-        ring_mid(1, 0, 1)
-        ring_mid(0, 2, 0)
-        ring_mid(0, 1, 0)
-        ring_last(1, 1)
+        ends(1, (2, 3))
+
+    def amid_zero(half):
+        if half == 0:
+            ends(1, (0, 1))
+        else:
+            mids(0, (4, 5, 2, 3))
 
     backward(0, got(3), up_zero, proj_zero, amid_zero)
     grads_a(0)
-    ring_end(1, 0, 1)
-    ring_end(0, 2, 0)
-    ring_end(0, 1, 0)
+    ends(0, (4, 5))
     d_first = backward_end(0)
     nat2[...] = tn(ton_ref[...], d_first.astype(BF)).astype(BF)
     for half in range(2):
@@ -550,54 +575,72 @@
                     16 * g : 16 * g + 16, 128 * lane_block : 128 * lane_block + 128
                 ]
     own = lane_start(1)
-    ring_mid(0, 0, 0)
-    ring_mid(0, 2, 1)
-    ring_mid(0, 1, 1)
-    ring_last(1, 0)
+    mids(0, (0, 1))
+    ends(0, (2, 3))
     finish(mixed_copies)
     natural = tn(son_ref[...], recv[2].reshape(4 * SLOT, C)).astype(BF)
-    mixed_ref[...] = natural.reshape(12, 16, C)[:, 0:WLON, :]
-    ring_end(0, 0, 0)
-    ring_end(0, 2, 1)
-    ring_end(0, 1, 1)
-    ring_mid(0, 0, 1)
-    ring_last(0, 2)
-    ring_last(0, 1)
+    mixed_ref[...] = natural.reshape(T // LEV, LEV, C)
+    stores = []
+
+    def store(src, dst):
+        stores.append(pltpu.make_async_copy(src, dst, out_sem.at[len(stores)]))
+        stores[-1].start()
+
+    store(mixed_ref, mixed_hbm)
+    lasts(1, range(6))
+    ends(0, (0, 1))
+    lasts(0, (4, 5, 2, 3))
+    store(oup_ref, oup_hbm)
+    store(odown_ref, odown_hbm)
     lane_finish(1, own)
     for half in range(2):
         rows = tn(came2[:, half].reshape(512, 128), spread_ref[...]).astype(BF)
         n = 8 if half == 0 else 4
         denc_ref[8 * half : 8 * half + n] = rows[0 : 16 * n].reshape(n, 16, 32 * WLON)
-    ring_end(0, 0, 1)
-    ring_last(0, 0)
+    store(denc_ref, denc_hbm)
+    lasts(0, (0, 1))
+    store(oqkv_ref, oqkv_hbm)
+    store(oproj_ref, oproj_hbm)
     for copy in sent:
         copy.wait_send()
+    finish(stores)
+
+
+def copies_kernel(*refs):
+    copies = [pltpu.make_async_copy(refs[n], refs[6 + n], refs[12].at[n]) for n in range(6)]
+    for copy in copies:
+        copy.start()
+    for copy in copies:
+        copy.wait()
 
 
 def layers(encoded, upstream, w_qkv, w_proj, w_up, w_down):
-    vmem = pl.BlockSpec(memory_space=pltpu.VMEM)
     hbm = pl.BlockSpec(memory_space=pl.ANY)
     dma = pltpu.SemaphoreType.DMA
     V = pltpu.VMEM
-    return pl.pallas_call(
+    shapes = (
+        jax.ShapeDtypeStruct((T // LEV, LEV, C), BF),
+        jax.ShapeDtypeStruct((12, 16, 32 * WLON), BF),
+        jax.ShapeDtypeStruct((12, 2, C), F32),
+        jax.ShapeDtypeStruct((2, 4, C), F32),
+        jax.ShapeDtypeStruct((2, 16, C), F32),
+        jax.ShapeDtypeStruct((2, 4, FF), F32),
+    )
+    results = pl.pallas_call(
         layers_kernel,
-        out_shape=(
-            jax.ShapeDtypeStruct((12, WLON, C), BF),
-            jax.ShapeDtypeStruct((12, 16, 32 * WLON), BF),
-            jax.ShapeDtypeStruct((12, 2, C), F32),
-            jax.ShapeDtypeStruct((2, 4, C), F32),
-            jax.ShapeDtypeStruct((2, 16, C), F32),
-            jax.ShapeDtypeStruct((2, 4, FF), F32),
-        ),
-        in_specs=[vmem] * 6 + [hbm] * 5,
-        out_specs=(vmem,) * 6,
+        out_shape=shapes,
+        in_specs=[hbm] * 11,
+        out_specs=(hbm,) * 6,
         scratch_shapes=[
+            V((12, 16, 32 * WLON), BF), V((T // LEV, LEV, C), BF), V((4 * SLOT, T), BF), V((T, 4 * SLOT), BF),
+            V((T, 12 * 16), BF), V((512, 32 * WLON), BF), dma((7,)),
+            *[V(shape.shape, shape.dtype) for shape in shapes], dma((6,)),
             V((2, C, 3 * C), BF), V((2, C, C), BF), V((2, C, FF), BF), V((2, FF, C), BF),
             dma((2, 4)),
-            V((1024, 1024), BF), dma, V((32, 2, 16, 128), BF), V((2, 4, 16, 1024), BF),
+            V((1024, 1024), BF), V((32, 2, 16, 128), BF), V((2, 4, 16, 1024), BF),
             V((32, 2, 16, 128), BF), V((32, 2, 16, 128), BF), dma((2, 32)), dma((2, 32)), dma((2,)),
             V((12 * 16, C), BF), V((2, 64, 1024), BF),
-            V((12, 16, C), BF), V((4, 4, SLOT, C), BF), V((4, 4, SLOT, C), BF),
+            V((4, 4, SLOT, C), BF), V((4, 4, SLOT, C), BF),
             dma((4, 4)), dma((4, 4)),
             V((2, T, C), F32), V((2, T, C), F32), V((2, T, C), BF), V((2, T, 128), F32),
             V((2, T, 3 * C), BF), V((2, HEADS, T, T), BF), V((2, T, C), BF),
@@ -607,25 +650,31 @@
             V((2, T, C), BF), V((2, T, C), BF), V((2, T, C), BF), V((2, T, FF), BF),
             V((2, 2, T, 384), BF), V((2, 2, T, 128), BF), V((2, 2, T, 512), BF), V((2, 2, T, 128), BF),
             dma((2, 12)), dma((2, 12)),
-            V((2, 3, 4, 4, 64, C), BF), V((2, 3, 2, 2, 64, C), BF), V((2, 3, 2, 2, 64, C), BF),
-            V((2, 3, 2, 4, 64, C), BF),
-            V((2, 3, 4, 64, C), BF), V((2, 3, 2, 32, C), BF), V((2, 3, 2, 32, C), BF),
-            V((2, 3, 2, 64, C), BF),
-            V((2, 3, 4, 16, C), F32), V((2, 3, 3, 16, C), F32),
-            dma((2, 3, 15)), dma((2, 3, 15)),
+            V((2, 6, 4, 4, 64, 256), BF), V((2, 6, 2, 2, 64, 256), BF), V((2, 6, 2, 2, 64, 256), BF),
+            V((2, 6, 2, 4, 64, 256), BF), V((2, 6, 4, 4, 16, 256), BF), V((2, 6, 16, 16, 256), BF),
+            dma((2, 6, 6)), dma((2, 6, 6)), dma((2, 6, 16)), dma((2, 6, 16)),
         ],
         compiler_params=pltpu.CompilerParams(
             collective_id=0, has_side_effects=True, vmem_limit_bytes=60 * 2**20
         ),
     )(encoded, upstream, *permutations(), w_qkv, w_proj, w_up, w_down)
+    return pl.pallas_call(
+        copies_kernel,
+        out_shape=shapes,
+        in_specs=[hbm] * 6,
+        out_specs=(hbm,) * 6,
+        scratch_shapes=[dma((6,))],
+    )(*results)
 
 
 def on_device(encoded, upstream, w_qkv, w_proj, w_up, w_down):
     mixed, dencoded, qkv, proj, up, down = layers(
-        encoded.reshape(12, 16, 32 * WLON), upstream.reshape(12, WLON, C), w_qkv, w_proj, w_up, w_down
+        encoded.reshape(12, 16, 32 * WLON),
+        upstream.transpose(1, 2, 0, 3).reshape(T // LEV, LEV, C),
+        w_qkv, w_proj, w_up, w_down,
     )
     return (
-        mixed.reshape(upstream.shape),
+        mixed.reshape(WLAT, WLON, LEV, C).transpose(2, 0, 1, 3),
         dencoded.reshape(encoded.shape),
         qkv.transpose(1, 2, 0),
         proj.swapaxes(1, 2),

time: 114 us -> 109 us (0.956)
  local copies, waits for them, and re-layouts: 10.6 us -> 0 us
  Pallas kernels: 102 us -> 107 us
    unnamed x7 -> x0, local copies, waits for them, and re-layouts: 10.6 us -> none
    pallas_call x1 -> x2, Pallas kernels: 102 us -> 107 us  [the longest x1 90.8 us: layers(): pl.pallas_call(layers_kernel, out_shape=shapes, in_specs=[hbm] * 11, out_...]
where the time goes in v4:
time: 109 us; the launch traced here: 108 us
  Pallas kernels  107 us (98%)
    pallas_call x1, Pallas kernels, layers(): pl.pallas_call(layers_kernel, out_shape=shapes, in_specs=[hbm] * 11, out_...  90.8 us
    pallas_call x1, Pallas kernels, layers(): pl.pallas_call(copies_kernel, out_shape=shapes, in_specs=[hbm] * 6, out_s...  16 us

profile of v4, /device:TPU:1, one launch (start us, length us, event | category | flops | bytes accessed | tf_op | source)
XLA Modules:
  0.0 107.6 jit_solution(2311041562759788868)
XLA Ops:
  0.6 90.8 %shard_map.154 = (bf16[72,2,512]{2,1,0:T(2,128)(2,1)}, bf16[12,16,384]{2,1,0:T(8,128)(2,1)}, f32[12,2,512]{2,1,0:T(2,128)}, f32[2,4,512]{2,1,0:T(4,128)}, f32[2,16,512]{2,1,0:T(8,128)}, /*index=5*/f32[2,4,2048]{2,1,0:T(4,128)}) custom-call(bf16[12,16,384]{2,1,0:T(8,128)(2,1)} %bitcast.12, bf16[72,2,512]{2,1,0:T(2,128)(2,1)} %bitcast.13, ...), custom_call_target="tpu_custom_call" | custom-call | tf_op jit(solution)/shard_map/pallas_call | solution.py:629
  91.4 16.0 %shard_map.155 = (bf16[72,2,512]{2,1,0:T(2,128)(2,1)}, bf16[12,16,384]{2,1,0:T(8,128)(2,1)}, f32[12,2,512]{2,1,0:T(2,128)}, f32[2,4,512]{2,1,0:T(4,128)}, f32[2,16,512]{2,1,0:T(8,128)}, /*index=5*/f32[2,4,2048]{2,1,0:T(4,128)}) custom-call(bf16[72,2,512]{2,1,0:T(2,128)(2,1)} %get-tuple-element.18.refs_0_, bf16[12,16,384]{2,1,0:T(8,128)(2,1)} %get-tuple-element.19.refs_1_, ...), custom_call_target="tpu_custom_call" | custom-call | tf_op jit(solution)/shard_map/pallas_call | solution.py:661

commit v5 on v4

--- a/solution.py
+++ b/solution.py
@@ -82,7 +82,7 @@
     enc_ref, up_ref, son_ref, tos_ref, ton_ref, spread_ref, in_sem,
     mixed_ref, denc_ref, oqkv_ref, oproj_ref, oup_ref, odown_ref, out_sem,
     wqkv, wproj, wup, wdown, wsem,
-    swap, leave, came, leave2, came2, lane_send, lane_recv, own_sem, nat2, turned, send, recv, send_sem, recv_sem,
+    swap, leave, came, leave2, came2, lane_send, lane_recv, nat2, turned, send, recv, send_sem, recv_sem,
     xs, n1h, n1, r1, us, ps, att, n2h, n2, r2, gp, hs, acc, eq, ep, eu, ed, dab,
     pn1, patt, pn2, phs, peq, pep, peu, ped, pair_send, pair_recv,
     part, fwd, fsum, side, plane_out, plane_in, ring_send, ring_recv, plane_send, plane_recv,
@@ -128,10 +128,10 @@
             fetches.append(fetch)
 
     barrier = pltpu.get_barrier_semaphore()
-    offsets = ((0, 1), (1, 0), (1, 1), (0, -1), (-1, 0), (-1, -1))
-    greeted = [device(di, dj) for di, dj in offsets]
-    greeted += [along(axis, steps) for axis in "xyz" for steps in (1, 2, 3)] + [partner]
-    greeted += [beside("x", dx, other, d) for other in "yz" for dx in (1, 2, 3) for d in (1, 2, 3)]
+    far = lambda xl, dy, dz: (lax.rem(i + 2, 4), lax.rem(y + dy, 4) * 8 + xl * 4 + lax.rem(z + dz, 4))
+    greeted = [device(1, 0), device(-1, 0), device(1, 1), device(-1, -1)]
+    greeted += [far(xl, 0, dz) for xl in range(2) for dz in range(4)]
+    greeted += [far(xl, dy, 0) for xl in range(2) for dy in (1, 2, 3)]
     for other in greeted:
         pl.semaphore_signal(barrier, inc=1, device_id=other, device_id_type=MESH)
 
@@ -155,7 +155,7 @@
         else:
             src, dst = leave2.at[to], came2.at[j]
         return pltpu.make_async_remote_copy(
-            src_ref=src, dst_ref=dst, send_sem=lane_send.at[event, step], recv_sem=lane_recv.at[event, step],
+            src_ref=src, dst_ref=dst, send_sem=lane_send.at[event], recv_sem=lane_recv.at[event],
             device_id=(i, to), device_id_type=MESH,
         )
 
@@ -168,30 +168,22 @@
             src, dst = leave.at[j], came.at[:, j // 8, :, mine]
         else:
             src, dst = leave2.at[j], came2.at[j]
-        own = pltpu.make_async_copy(src, dst, own_sem.at[event])
-        own.start()
-        return own
-
-    def lane_finish(event, own):
-        own.wait()
-
-        @pl.loop(1, nlon)
-        def _(step):
-            lane_copy(step, event).wait()
-
-    own = lane_start(0)
-
-    def remote(src, dst, sems, index, to):
-        copy = pltpu.make_async_remote_copy(
-            src_ref=src, dst_ref=dst, send_sem=sems[0].at[index], recv_sem=sems[1].at[index],
-            device_id=to, device_id_type=MESH,
-        )
-        copy.start()
-        sent.append(copy)
-        return copy
-
-    sent = []
-    pairs = {}
+        pltpu.make_async_copy(src, dst, lane_recv.at[event]).start()
+
+    def lane_finish(event):
+        await_bytes((came, came2)[event], lane_recv.at[event])
+        await_bytes((leave, leave2)[event].at[pl.ds(0, 31)], lane_send.at[event])
+
+    lane_start(0)
+
+    def remote(src, dst, sems, to):
+        pltpu.make_async_remote_copy(
+            src_ref=src, dst_ref=dst, send_sem=sems[0], recv_sem=sems[1], device_id=to, device_id_type=MESH
+        ).start()
+
+    def await_bytes(like, sem):
+        pltpu.make_async_copy(like, like, sem).wait()
+
     wide = {"eq": 384, "ep": 128, "eu": 512, "ed": 128}
     whole = {"n1": (n1, pn1), "att": (att, patt), "n2": (n2, pn2), "hs": (hs, phs)}
     cut = {"eq": (eq, peq), "ep": (ep, pep), "eu": (eu, peu), "ed": (ed, ped)}
@@ -200,27 +192,27 @@
         width = wide[name]
         return pl.ds(pl.multiple_of((2 * hi + owner) * width, width), width)
 
+    names = ("n1", "att", "n2", "hs", "eq", "ep", "eu", "ed")
+
     def give(k, name):
-        sems = (pair_send, pair_recv)
+        sems = (pair_send.at[k, names.index(name)], pair_recv.at[k, names.index(name)])
         if name in whole:
             src, dst = whole[name]
-            index = list(whole).index(name)
-            pairs[k, name] = [remote(src.at[k], dst.at[k], sems, (k, index), partner)]
+            remote(src.at[k], dst.at[k], sems, partner)
         else:
             src, dst = cut[name]
-            index = 4 + 2 * list(cut).index(name)
-            pairs[k, name] = [
-                remote(src.at[k, :, columns(name, hi, 1 - core)], dst.at[k, hi], sems, (k, index + hi), partner)
-                for hi in range(2)
-            ]
+            for hi in range(2):
+                remote(src.at[k, :, columns(name, hi, 1 - core)], dst.at[k, hi], sems, partner)
+
+    def taken(k, name, sems):
+        dst = (whole[name] if name in whole else cut[name])[1]
+        await_bytes(dst.at[k], sems.at[k, names.index(name)])
 
     def take(k, name):
-        for copy in pairs[k, name]:
-            copy.wait_recv()
+        taken(k, name, pair_recv)
 
     orders = ("xyz", "yxz", "zyx", "zyx", "xyz", "yxz")
     where = {"x": x, "y": y, "z": z}
-    rings = {}
 
     def chunk(k, p, t, half):
         return part.at[k, p, lax.rem(t + 4, 4), pl.ds(2 * half, 2)]
@@ -232,39 +224,35 @@
         axis = orders[p][0]
         t = where[axis]
         after, before = along(axis, 1), along(axis, -1)
-        sems = (ring_send, ring_recv)
-        rings[k, p] = [
-            remote(chunk(k, p, t + 2, 0), fwd.at[k, p, 0], sems, (k, p, 0), after),
-            remote(chunk(k, p, t + 2, 1), fwd.at[k, p, 1], sems, (k, p, 1), before),
-            remote(chunk(k, p, t + 1, 1), side.at[k, p, 0, pl.ds(2, 2)], sems, (k, p, 2), after),
-            remote(chunk(k, p, t - 1, 0), side.at[k, p, 1, pl.ds(0, 2)], sems, (k, p, 3), before),
-        ]
+        out = ring_send.at[k, p]
+        remote(chunk(k, p, t + 2, 0), fwd.at[k, p, 0], (out, ring_recv.at[k, p, 0]), after)
+        remote(chunk(k, p, t + 2, 1), fwd.at[k, p, 1], (out, ring_recv.at[k, p, 1]), before)
+        remote(chunk(k, p, t + 1, 1), side.at[k, p, 0, pl.ds(2, 2)], (out, ring_recv.at[k, p, 2]), after)
+        remote(chunk(k, p, t - 1, 0), side.at[k, p, 1, pl.ds(0, 2)], (out, ring_recv.at[k, p, 2]), before)
 
     def ring_mid(k, p):
         axis = orders[p][0]
         t = where[axis]
         after, before = along(axis, 1), along(axis, -1)
-        copies = rings[k, p]
-        sems = (ring_send, ring_recv)
-        copies[0].wait_recv()
+        sems = (ring_send.at[k, p], ring_recv.at[k, p, 2])
+        await_bytes(fwd.at[k, p, 0], ring_recv.at[k, p, 0])
         fsum[k, p, 0] = (f32(fwd.at[k, p, 0]) + f32(chunk(k, p, t + 1, 0))).astype(BF)
-        copies.append(remote(fsum.at[k, p, 0], side.at[k, p, 0, pl.ds(0, 2)], sems, (k, p, 4), after))
-        copies[1].wait_recv()
+        remote(fsum.at[k, p, 0], side.at[k, p, 0, pl.ds(0, 2)], sems, after)
+        await_bytes(fwd.at[k, p, 1], ring_recv.at[k, p, 1])
         fsum[k, p, 1] = (f32(fwd.at[k, p, 1]) + f32(chunk(k, p, t - 1, 1))).astype(BF)
-        copies.append(remote(fsum.at[k, p, 1], side.at[k, p, 1, pl.ds(2, 2)], sems, (k, p, 5), before))
+        remote(fsum.at[k, p, 1], side.at[k, p, 1, pl.ds(2, 2)], sems, before)
 
     def plane_copy(k, p, step):
         _, second, third = orders[p]
         d2, d3 = step // 4, lax.rem(step, 4)
         src = plane_out.at[k, p, lax.rem(where[second] + d2, 4), lax.rem(where[third] + d3, 4)]
         return pltpu.make_async_remote_copy(
-            src_ref=src, dst_ref=plane_in.at[k, p, step], send_sem=plane_send.at[k, p, step],
-            recv_sem=plane_recv.at[k, p, step], device_id=beside(second, d2, third, d3), device_id_type=MESH,
+            src_ref=src, dst_ref=plane_in.at[k, p, step], send_sem=plane_send.at[k, p],
+            recv_sem=plane_recv.at[k, p], device_id=beside(second, d2, third, d3), device_id_type=MESH,
         )
 
     def ring_end(k, p):
-        for copy in rings[k, p][2:]:
-            copy.wait_recv()
+        await_bytes(side.at[k, p], ring_recv.at[k, p, 2])
         t = where[orders[p][0]]
         total = f32(part.at[k, p, t]) + f32(side.at[k, p, 0]) + f32(side.at[k, p, 1])
         for s2 in range(4):
@@ -284,10 +272,7 @@
             plane_copy(k, p, step).start()
 
     def ring_last(k, p):
-        @pl.loop(1, 16)
-        def _(step):
-            plane_copy(k, p, step).wait()
-
+        await_bytes(plane_in.at[k, p, pl.ds(1, 15)], plane_recv.at[k, p])
         _, second, third = orders[p]
         total = f32(plane_out.at[k, p, where[second], where[third]])
         for step in range(1, 16):
@@ -350,25 +335,17 @@
         ring_start(k, 5)
 
     def exchange(event, forward):
-        copies = []
         for q in range(4):
             a, b = q // 2, q % 2
             di, dj = (a - 1, b - 1) if forward else (a, b)
             if (di, dj) == (0, 0):
                 recv[event, 3 - q] = send[event, q]
             else:
-                copy = pltpu.make_async_remote_copy(
-                    src_ref=send.at[event, q], dst_ref=recv.at[event, 3 - q],
-                    send_sem=send_sem.at[event, q], recv_sem=recv_sem.at[event, 3 - q],
-                    device_id=device(di, dj), device_id_type=MESH,
-                )
-                copy.start()
-                copies.append(copy)
-        return copies
-
-    def finish(copies):
-        for copy in copies:
-            copy.wait()
+                sems = (send_sem.at[event], recv_sem.at[event])
+                remote(send.at[event, q], recv.at[event, 3 - q], sems, device(di, dj))
+
+    def arrive(event):
+        await_bytes(recv.at[event, pl.ds(0, 3)], recv_sem.at[event])
 
     def put(event, tokens):
         send[event] = tn(tos_ref[...], tokens).astype(BF).reshape(4, SLOT, C)
@@ -379,7 +356,7 @@
     for name in ("up", "son", "tos", "ton"):
         inputs[name].wait()
     send[0] = nn(son_ref[...], up_ref[...].reshape(T, C)).astype(BF).reshape(4, SLOT, C)
-    up_copies = exchange(0, True)
+    exchange(0, True)
 
     lane = lax.broadcasted_iota(jnp.int32, (1, 128), 1)
     head_mask = [((lane >= 32 * s) & (lane < 32 * s + 32)).astype(BF) for s in range(4)]
@@ -387,6 +364,14 @@
     half_s = lax.broadcasted_iota(jnp.int32, (T, T), 1) < T // 2
     apart = jnp.where(half_t == half_s, 0.0, 1.0).astype(F32)
     last = jnp.where(i == nlat - 1, 1.0, 0.0).astype(F32)
+    extra = [((lane == (32 * s + 64) % 128) | (lane == (32 * s + 64) % 128 + 1)) for s in range(4)]
+    inside = [(lane >= 32 * s) & (lane < 32 * s + 32) for s in range(4)]
+    first_extra = lax.rem(lane, 32) == 0
+    gather_rows = lax.broadcasted_iota(jnp.int32, (128, 128), 0) // 32
+    gather_cols = lax.broadcasted_iota(jnp.int32, (128, 128), 1)
+    gather = jnp.where(
+        (lax.rem(gather_cols, 32) < 2) & (lax.rem(gather_cols // 32 + 2, 4) == gather_rows), 1.0, 0.0
+    ).astype(BF)
 
     def forward(k, x):
         xs[k] = x
@@ -413,7 +398,7 @@
                 e = jnp.exp(nt(q * head_mask[s], key) * (32**-0.5))
                 if k == 1:
                     e = e * (1.0 - last * apart)
-                p = (e / jnp.sum(e, -1, keepdims=True)).astype(BF)
+                p = ((e * (1.0 / (0.25 * jnp.sum(e, -1, keepdims=True)))) * 0.25).astype(BF)
                 ps[k, g * 4 + s] = p
                 total += nn(p, v * head_mask[s])
             att[k, :, pl.ds(pl.multiple_of(g * 128, 128), 128)] = total.astype(BF)
@@ -475,18 +460,23 @@
             dq = jnp.zeros((T, 128), F32)
             dk = jnp.zeros((T, 128), F32)
             dv = jnp.zeros((T, 128), F32)
+            prod = da.astype(F32) * att[k, :, at(0)].astype(F32)
+            high = prod.astype(BF)
+            low = (prod - high.astype(F32)).astype(BF)
+            sums = nn(high, gather) + nn(low, gather)
+            sums_high = sums.astype(BF).astype(F32)
+            sums = jnp.where(first_extra, sums_high, sums - sums_high).astype(BF)
             for s in range(4):
                 p = ps[k, g * 4 + s]
                 dah = da * head_mask[s]
-                dp = nt(dah, v).astype(BF).astype(F32)
+                with_sums = jnp.where(inside[s], da, jnp.where(extra[s], sums, jnp.zeros_like(sums)))
+                dp = nt(with_sums, jnp.where(extra[s], -jnp.ones_like(v), v))
                 dv += tn(p, dah)
-                pf = p.astype(F32)
-                ds = pf * (dp - jnp.sum(dp * pf, -1, keepdims=True))
-                ds = (ds * (32**-0.5)).astype(BF)
+                ds = (p.astype(F32) * dp).astype(BF)
                 dq += nn(ds, key * head_mask[s])
                 dk += tn(ds, q * head_mask[s])
-            eq[k, :, at(0)] = dq.astype(BF)
-            eq[k, :, at(1)] = dk.astype(BF)
+            eq[k, :, at(0)] = (dq * (32**-0.5)).astype(BF)
+            eq[k, :, at(1)] = (dk * (32**-0.5)).astype(BF)
             eq[k, :, at(2)] = dv.astype(BF)
 
         for half in range(2):
@@ -502,7 +492,7 @@
         pass
 
     inputs["swap"].wait()
-    lane_finish(0, own)
+    lane_finish(0)
     for half in range(2):
         moved = nn(came[half].reshape(64, 1024), swap[...]).astype(BF)
         for lr in range(8 if half == 0 else 4):
@@ -511,11 +501,12 @@
                 nat2[at] = moved[16 * g : 16 * g + 16, 128 * lr : 128 * lr + 128]
     first = forward(0, nn(ton_ref[...], nat2[...]))
     put(1, first.astype(BF))
-    finish(exchange(1, True))
+    exchange(1, True)
+    arrive(1)
     second = forward(1, got(1))
     put(2, second.astype(BF))
-    mixed_copies = exchange(2, False)
-    finish(up_copies)
+    exchange(2, False)
+    arrive(0)
 
     def mids(k, parts):
         for p in parts:
@@ -536,10 +527,10 @@
     backward(1, got(0), nothing, nothing, amid_one)
     d_second = backward_end(1)
     put(3, d_second.astype(BF))
-    mid_copies = exchange(3, False)
+    exchange(3, False)
     grads_a(1)
     mids(1, (2, 3))
-    finish(mid_copies)
+    arrive(3)
 
     def up_zero():
         ends(1, (4, 5))
@@ -574,10 +565,10 @@
                 leave2[8 * g + lane_block, half] = moved[
                     16 * g : 16 * g + 16, 128 * lane_block : 128 * lane_block + 128
                 ]
-    own = lane_start(1)
+    lane_start(1)
     mids(0, (0, 1))
     ends(0, (2, 3))
-    finish(mixed_copies)
+    arrive(2)
     natural = tn(son_ref[...], recv[2].reshape(4 * SLOT, C)).astype(BF)
     mixed_ref[...] = natural.reshape(T // LEV, LEV, C)
     stores = []
@@ -592,7 +583,7 @@
     lasts(0, (4, 5, 2, 3))
     store(oup_ref, oup_hbm)
     store(odown_ref, odown_hbm)
-    lane_finish(1, own)
+    lane_finish(1)
     for half in range(2):
         rows = tn(came2[:, half].reshape(512, 128), spread_ref[...]).astype(BF)
         n = 8 if half == 0 else 4
@@ -601,21 +592,26 @@
     lasts(0, (0, 1))
     store(oqkv_ref, oqkv_hbm)
     store(oproj_ref, oproj_hbm)
-    for copy in sent:
-        copy.wait_send()
-    finish(stores)
+    for event in range(4):
+        await_bytes(send.at[event, pl.ds(0, 3)], send_sem.at[event])
+    for k in range(2):
+        for name in names:
+            taken(k, name, pair_send)
+        for p in range(6):
+            await_bytes(part.at[k, p, pl.ds(0, 3)], ring_send.at[k, p])
+            await_bytes(plane_in.at[k, p, pl.ds(1, 15)], plane_send.at[k, p])
+    for copy in stores:
+        copy.wait()
 
 
 def copies_kernel(*refs):
-    copies = [pltpu.make_async_copy(refs[n], refs[6 + n], refs[12].at[n]) for n in range(6)]
-    for copy in copies:
-        copy.start()
-    for copy in copies:
-        copy.wait()
+    for n in range(6):
+        refs[6 + n][...] = refs[n][...]
 
 
 def layers(encoded, upstream, w_qkv, w_proj, w_up, w_down):
     hbm = pl.BlockSpec(memory_space=pl.ANY)
+    vmem = pl.BlockSpec(memory_space=pltpu.VMEM)
     dma = pltpu.SemaphoreType.DMA
     V = pltpu.VMEM
     shapes = (
@@ -638,10 +634,10 @@
             V((2, C, 3 * C), BF), V((2, C, C), BF), V((2, C, FF), BF), V((2, FF, C), BF),
             dma((2, 4)),
             V((1024, 1024), BF), V((32, 2, 16, 128), BF), V((2, 4, 16, 1024), BF),
-            V((32, 2, 16, 128), BF), V((32, 2, 16, 128), BF), dma((2, 32)), dma((2, 32)), dma((2,)),
+            V((32, 2, 16, 128), BF), V((32, 2, 16, 128), BF), dma((2,)), dma((2,)),
             V((12 * 16, C), BF), V((2, 64, 1024), BF),
             V((4, 4, SLOT, C), BF), V((4, 4, SLOT, C), BF),
-            dma((4, 4)), dma((4, 4)),
+            dma((4,)), dma((4,)),
             V((2, T, C), F32), V((2, T, C), F32), V((2, T, C), BF), V((2, T, 128), F32),
             V((2, T, 3 * C), BF), V((2, HEADS, T, T), BF), V((2, T, C), BF),
             V((2, T, C), F32), V((2, T, C), BF), V((2, T, 128), F32),
@@ -649,10 +645,10 @@
             V((2, T, 3 * C), BF), V((2, T, C), BF), V((2, T, FF), BF), V((2, T, C), BF), V((T, C), BF),
             V((2, T, C), BF), V((2, T, C), BF), V((2, T, C), BF), V((2, T, FF), BF),
             V((2, 2, T, 384), BF), V((2, 2, T, 128), BF), V((2, 2, T, 512), BF), V((2, 2, T, 128), BF),
-            dma((2, 12)), dma((2, 12)),
+            dma((2, 8)), dma((2, 8)),
             V((2, 6, 4, 4, 64, 256), BF), V((2, 6, 2, 2, 64, 256), BF), V((2, 6, 2, 2, 64, 256), BF),
             V((2, 6, 2, 4, 64, 256), BF), V((2, 6, 4, 4, 16, 256), BF), V((2, 6, 16, 16, 256), BF),
-            dma((2, 6, 6)), dma((2, 6, 6)), dma((2, 6, 16)), dma((2, 6, 16)),
+            dma((2, 6)), dma((2, 6, 3)), dma((2, 6)), dma((2, 6)),
         ],
         compiler_params=pltpu.CompilerParams(
             collective_id=0, has_side_effects=True, vmem_limit_bytes=60 * 2**20
@@ -661,9 +657,8 @@
     return pl.pallas_call(
         copies_kernel,
         out_shape=shapes,
-        in_specs=[hbm] * 6,
-        out_specs=(hbm,) * 6,
-        scratch_shapes=[dma((6,))],
+        in_specs=[vmem] * 6,
+        out_specs=(vmem,) * 6,
     )(*results)
 
 

time: 109 us -> 88.2 us (0.81); the launches traced: 108 us -> 88 us
  Pallas kernels: 107 us -> 87.3 us
    pallas_call x1, Pallas kernels: 16 us -> 1.84 us  [layers(): pl.pallas_call(copies_kernel, out_shape=shapes, in_specs=[vmem] * 6, out_...]
    pallas_call x1, Pallas kernels: 90.8 us -> 85.5 us  [layers(): pl.pallas_call(layers_kernel, out_shape=shapes, in_specs=[hbm] * 11, out_...]
where the time goes in v5:
time: 88.2 us; the launch traced here: 88 us
  Pallas kernels  87.3 us (99%)
    pallas_call x1, Pallas kernels, layers(): pl.pallas_call(layers_kernel, out_shape=shapes, in_specs=[hbm] * 11, out_...  85.5 us
    pallas_call x1, Pallas kernels, layers(): pl.pallas_call(copies_kernel, out_shape=shapes, in_specs=[vmem] * 6, out_...  1.84 us

profile of v5, /device:TPU:1, one launch (start us, length us, event | category | flops | bytes accessed | tf_op | source)
XLA Modules:
  0.0 88.0 jit_solution(17843964022399311119)
XLA Ops:
  0.6 85.5 %shard_map.154 = (bf16[72,2,512]{2,1,0:T(2,128)(2,1)}, bf16[12,16,384]{2,1,0:T(8,128)(2,1)}, f32[12,2,512]{2,1,0:T(2,128)}, f32[2,4,512]{2,1,0:T(4,128)}, f32[2,16,512]{2,1,0:T(8,128)}, /*index=5*/f32[2,4,2048]{2,1,0:T(4,128)}) custom-call(bf16[12,16,384]{2,1,0:T(8,128)(2,1)} %bitcast.12, bf16[72,2,512]{2,1,0:T(2,128)(2,1)} %bitcast.13, ...), custom_call_target="tpu_custom_call" | custom-call | tf_op jit(solution)/shard_map/pallas_call | solution.py:625
  86.1 1.8 %shard_map.155 = (bf16[72,2,512]{2,1,0:T(2,128)(2,1)}, bf16[12,16,384]{2,1,0:T(8,128)(2,1)}, f32[12,2,512]{2,1,0:T(2,128)}, f32[2,4,512]{2,1,0:T(4,128)}, f32[2,16,512]{2,1,0:T(8,128)}, /*index=5*/f32[2,4,2048]{2,1,0:T(4,128)}) custom-call(bf16[72,2,512]{2,1,0:T(2,128)(2,1)} %get-tuple-element.18.refs_0_, bf16[12,16,384]{2,1,0:T(8,128)(2,1)} %get-tuple-element.19.refs_1_, ...), custom_call_target="tpu_custom_call" | custom-call | tf_op jit(solution)/shard_map/pallas_call | solution.py:657

commit v6 on v5

--- a/solution.py
+++ b/solution.py
@@ -83,7 +83,7 @@
     mixed_ref, denc_ref, oqkv_ref, oproj_ref, oup_ref, odown_ref, out_sem,
     wqkv, wproj, wup, wdown, wsem,
     swap, leave, came, leave2, came2, lane_send, lane_recv, nat2, turned, send, recv, send_sem, recv_sem,
-    xs, n1h, n1, r1, us, ps, att, n2h, n2, r2, gp, hs, acc, eq, ep, eu, ed, dab,
+    xs, n1h, n1, r1, us, ps, att, seen, n2h, n2, r2, gp, hs, acc, eq, ep, eu, ed, dab,
     pn1, patt, pn2, phs, peq, pep, peu, ped, pair_send, pair_recv,
     part, fwd, fsum, side, plane_out, plane_in, ring_send, ring_recv, plane_send, plane_recv,
 ):
@@ -362,16 +362,13 @@
     head_mask = [((lane >= 32 * s) & (lane < 32 * s + 32)).astype(BF) for s in range(4)]
     half_t = lax.broadcasted_iota(jnp.int32, (T, T), 0) < T // 2
     half_s = lax.broadcasted_iota(jnp.int32, (T, T), 1) < T // 2
-    apart = jnp.where(half_t == half_s, 0.0, 1.0).astype(F32)
-    last = jnp.where(i == nlat - 1, 1.0, 0.0).astype(F32)
-    extra = [((lane == (32 * s + 64) % 128) | (lane == (32 * s + 64) % 128 + 1)) for s in range(4)]
+    one = jnp.where((i == nlat - 1) & (half_t != half_s), 0.0, 1.0).astype(F32)
+    for s in range(4):
+        seen[T * s : T * s + T] = one
     inside = [(lane >= 32 * s) & (lane < 32 * s + 32) for s in range(4)]
-    first_extra = lax.rem(lane, 32) == 0
-    gather_rows = lax.broadcasted_iota(jnp.int32, (128, 128), 0) // 32
-    gather_cols = lax.broadcasted_iota(jnp.int32, (128, 128), 1)
-    gather = jnp.where(
-        (lax.rem(gather_cols, 32) < 2) & (lax.rem(gather_cols // 32 + 2, 4) == gather_rows), 1.0, 0.0
-    ).astype(BF)
+    two = lax.broadcasted_iota(jnp.int32, (128, 128), 1) < 2
+    ones_two = jnp.where(two, 1.0, 0.0).astype(BF)
+    minus_two = jnp.where(lax.broadcasted_iota(jnp.int32, (T, 128), 1) < 2, -1.0, 0.0).astype(BF)
 
     def forward(k, x):
         xs[k] = x
@@ -382,9 +379,8 @@
         give(k, "n1")
         fetches[4 * k].wait()
 
-        @pl.loop(0, 3)
-        def _(s):
-            cols = pl.ds(pl.multiple_of(s * C, C), C)
+        for s in range(3):
+            cols = slice(s * C, s * C + C)
             us[k, :, cols] = nn(n1[k], wqkv[k, :, cols]).astype(BF)
 
         @pl.loop(0, 4)
@@ -393,14 +389,16 @@
                 return us[k, :, pl.ds(pl.multiple_of(w * C + g * 128, 128), 128)]
 
             q, key, v = part(0), part(1), part(2)
+            stacked = jnp.concatenate([q * m for m in head_mask], 0)
+            e = jnp.exp2(nt(stacked, key) * (32**-0.5 / np.log(2.0)))
+            if k == 1:
+                e = e * seen[...]
+            p = ((e * (1.0 / (0.25 * jnp.sum(e, -1, keepdims=True)))) * 0.25).astype(BF)
+            ps[k, g] = p
+            out = nn(p, v)
             total = jnp.zeros((T, 128), F32)
             for s in range(4):
-                e = jnp.exp(nt(q * head_mask[s], key) * (32**-0.5))
-                if k == 1:
-                    e = e * (1.0 - last * apart)
-                p = ((e * (1.0 / (0.25 * jnp.sum(e, -1, keepdims=True)))) * 0.25).astype(BF)
-                ps[k, g * 4 + s] = p
-                total += nn(p, v * head_mask[s])
+                total += jnp.where(inside[s], out[T * s : T * s + T], 0.0)
             att[k, :, pl.ds(pl.multiple_of(g * 128, 128), 128)] = total.astype(BF)
 
         give(k, "att")
@@ -415,9 +413,8 @@
         fetches[4 * k + 2].wait()
         fetches[4 * k + 3].wait()
 
-        @pl.loop(0, 4)
-        def _(s):
-            cols = pl.ds(pl.multiple_of(s * C, C), C)
+        for s in range(4):
+            cols = slice(s * C, s * C + C)
             z = nn(n2[k], wup[k, :, cols])
             cdf = 0.5 * (1.0 + lax.erf(z * (2.0**-0.5)))
             gp[k, :, cols] = cdf + z * (jnp.exp(-0.5 * z * z) * ((2.0 * np.pi) ** -0.5))
@@ -433,9 +430,8 @@
         ed[k] = ct.astype(BF)
         give(k, "ed")
 
-        @pl.loop(0, 4)
-        def _(s):
-            cols = pl.ds(pl.multiple_of(s * C, C), C)
+        for s in range(4):
+            cols = slice(s * C, s * C + C)
             dh = nt(ed[k], wdown[k, cols, :]).astype(BF).astype(F32)
             eu[k, :, cols] = (dh * gp[k, :, cols]).astype(BF)
 
@@ -457,24 +453,23 @@
 
             q, key, v = us[k, :, at(0)], us[k, :, at(1)], us[k, :, at(2)]
             da = dab[:, at(0)]
-            dq = jnp.zeros((T, 128), F32)
-            dk = jnp.zeros((T, 128), F32)
-            dv = jnp.zeros((T, 128), F32)
             prod = da.astype(F32) * att[k, :, at(0)].astype(F32)
             high = prod.astype(BF)
             low = (prod - high.astype(F32)).astype(BF)
-            sums = nn(high, gather) + nn(low, gather)
+            stacked_da = jnp.concatenate([da * m for m in head_mask], 0)
+            sums = nn(jnp.concatenate([high * m for m in head_mask], 0), ones_two)
+            sums += nn(jnp.concatenate([low * m for m in head_mask], 0), ones_two)
             sums_high = sums.astype(BF).astype(F32)
-            sums = jnp.where(first_extra, sums_high, sums - sums_high).astype(BF)
+            sums = jnp.where(lane == 0, sums_high, sums - sums_high).astype(BF)
+            p = ps[k, g]
+            dp = nt(jnp.concatenate([stacked_da, sums], 1), jnp.concatenate([v, minus_two], 1))
+            ds = (p.astype(F32) * dp).astype(BF)
+            dv = tn(p, stacked_da)
+            dk = tn(ds, jnp.concatenate([q * m for m in head_mask], 0))
+            out = nn(ds, key)
+            dq = jnp.zeros((T, 128), F32)
             for s in range(4):
-                p = ps[k, g * 4 + s]
-                dah = da * head_mask[s]
-                with_sums = jnp.where(inside[s], da, jnp.where(extra[s], sums, jnp.zeros_like(sums)))
-                dp = nt(with_sums, jnp.where(extra[s], -jnp.ones_like(v), v))
-                dv += tn(p, dah)
-                ds = (p.astype(F32) * dp).astype(BF)
-                dq += nn(ds, key * head_mask[s])
-                dk += tn(ds, q * head_mask[s])
+                dq += jnp.where(inside[s], out[T * s : T * s + T], 0.0)
             eq[k, :, at(0)] = (dq * (32**-0.5)).astype(BF)
             eq[k, :, at(1)] = (dk * (32**-0.5)).astype(BF)
             eq[k, :, at(2)] = dv.astype(BF)
@@ -639,7 +634,8 @@
             V((4, 4, SLOT, C), BF), V((4, 4, SLOT, C), BF),
             dma((4,)), dma((4,)),
             V((2, T, C), F32), V((2, T, C), F32), V((2, T, C), BF), V((2, T, 128), F32),
-            V((2, T, 3 * C), BF), V((2, HEADS, T, T), BF), V((2, T, C), BF),
+            V((2, T, 3 * C), BF), V((2, 4, 4 * T, T), BF), V((2, T, C), BF),
+            V((4 * T, T), F32),
             V((2, T, C), F32), V((2, T, C), BF), V((2, T, 128), F32),
             V((2, T, FF), F32), V((2, T, FF), BF), V((T, C), F32),
             V((2, T, 3 * C), BF), V((2, T, C), BF), V((2, T, FF), BF), V((2, T, C), BF), V((T, C), BF),

time: 88.2 us -> 84.5 us (0.958)
  Pallas kernels: 87.3 us -> 82.8 us
    pallas_call x1, Pallas kernels: 85.5 us -> 81 us  [layers(): pl.pallas_call(layers_kernel, out_shape=shapes, in_specs=[hbm] * 11, out_...]
where the time goes in v6:
time: 84.5 us; the launch traced here: 83.4 us
  Pallas kernels  82.8 us (98%)
    pallas_call x1, Pallas kernels, layers(): pl.pallas_call(layers_kernel, out_shape=shapes, in_specs=[hbm] * 11, out_...  81 us
    pallas_call x1, Pallas kernels, layers(): pl.pallas_call(copies_kernel, out_shape=shapes, in_specs=[vmem] * 6, out_...  1.84 us

profile of v6, /device:TPU:1, one launch (start us, length us, event | category | flops | bytes accessed | tf_op | source)
XLA Modules:
  0.0 83.4 jit_solution(13221433211578597789)
XLA Ops:
  0.6 81.0 %shard_map.154 = (bf16[72,2,512]{2,1,0:T(2,128)(2,1)}, bf16[12,16,384]{2,1,0:T(8,128)(2,1)}, f32[12,2,512]{2,1,0:T(2,128)}, f32[2,4,512]{2,1,0:T(4,128)}, f32[2,16,512]{2,1,0:T(8,128)}, /*index=5*/f32[2,4,2048]{2,1,0:T(4,128)}) custom-call(bf16[12,16,384]{2,1,0:T(8,128)(2,1)} %bitcast.12, bf16[72,2,512]{2,1,0:T(2,128)(2,1)} %bitcast.13, ...), custom_call_target="tpu_custom_call" | custom-call | tf_op jit(solution)/shard_map/pallas_call | solution.py:620
  81.6 1.8 %shard_map.155 = (bf16[72,2,512]{2,1,0:T(2,128)(2,1)}, bf16[12,16,384]{2,1,0:T(8,128)(2,1)}, f32[12,2,512]{2,1,0:T(2,128)}, f32[2,4,512]{2,1,0:T(4,128)}, f32[2,16,512]{2,1,0:T(8,128)}, /*index=5*/f32[2,4,2048]{2,1,0:T(4,128)}) custom-call(bf16[72,2,512]{2,1,0:T(2,128)(2,1)} %get-tuple-element.18.refs_0_, bf16[12,16,384]{2,1,0:T(8,128)(2,1)} %get-tuple-element.19.refs_1_, ...), custom_call_target="tpu_custom_call" | custom-call | tf_op jit(solution)/shard_map/pallas_call | solution.py:653

commit v7 on v6

--- a/solution.py
+++ b/solution.py
@@ -119,13 +119,11 @@
         )
     ):
         inputs[name] = pltpu.make_async_copy(src, dst, in_sem.at[at])
-        inputs[name].start()
-    fetches = []
-    for k in range(2):
-        for w, (src, dst) in enumerate(weights):
-            fetch = pltpu.make_async_copy(src.at[k], dst.at[k], wsem.at[k, w])
-            fetch.start()
-            fetches.append(fetch)
+    inputs["enc"].start()
+    inputs["spread"].start()
+    fetches = [
+        pltpu.make_async_copy(src.at[k], dst.at[k], wsem.at[k, w]) for k in range(2) for w, (src, dst) in enumerate(weights)
+    ]
 
     barrier = pltpu.get_barrier_semaphore()
     far = lambda xl, dy, dz: (lax.rem(i + 2, 4), lax.rem(y + dy, 4) * 8 + xl * 4 + lax.rem(z + dz, 4))
@@ -138,6 +136,11 @@
     @pl.loop(1, nlon)
     def _(step):
         pl.semaphore_signal(barrier, inc=1, device_id=device(0, step), device_id_type=MESH)
+
+    for name in ("up", "son", "tos", "ton", "swap"):
+        inputs[name].start()
+    for fetch in fetches:
+        fetch.start()
 
     inputs["enc"].wait()
     inputs["spread"].wait()
@@ -211,7 +214,7 @@
     def take(k, name):
         taken(k, name, pair_recv)
 
-    orders = ("xyz", "yxz", "zyx", "zyx", "xyz", "yxz")
+    orders = ("xyz", "xyz", "yxz", "yxz", "zyx", "zyx")
     where = {"x": x, "y": y, "z": z}
 
     def chunk(k, p, t, half):
@@ -242,14 +245,30 @@
         fsum[k, p, 1] = (f32(fwd.at[k, p, 1]) + f32(chunk(k, p, t - 1, 1))).astype(BF)
         remote(fsum.at[k, p, 1], side.at[k, p, 1, pl.ds(2, 2)], sems, before)
 
-    def plane_copy(k, p, step):
+    def plane_copy(k, p, count, step):
         _, second, third = orders[p]
         d2, d3 = step // 4, lax.rem(step, 4)
-        src = plane_out.at[k, p, lax.rem(where[second] + d2, 4), lax.rem(where[third] + d3, 4)]
+        held = pl.ds(p % 2, count)
+        src = plane_out.at[k, p // 2, lax.rem(where[second] + d2, 4), lax.rem(where[third] + d3, 4), held]
         return pltpu.make_async_remote_copy(
-            src_ref=src, dst_ref=plane_in.at[k, p, step], send_sem=plane_send.at[k, p],
+            src_ref=src, dst_ref=plane_in.at[k, p // 2, step, held], send_sem=plane_send.at[k, p],
             recv_sem=plane_recv.at[k, p], device_id=beside(second, d2, third, d3), device_id_type=MESH,
         )
+
+    def plane_start(k, p, count):
+        planes.append((k, p, count))
+
+        @pl.loop(1, 16)
+        def _(step):
+            plane_copy(k, p, count, step).start()
+
+    planes = []
+
+    def plane_bytes(k, p, count):
+        return plane_in.at[k, p // 2, pl.ds(1, 15), pl.ds(p % 2, count)]
+
+    def plane_arrive(k, p, count):
+        await_bytes(plane_bytes(k, p, count), plane_recv.at[k, p])
 
     def ring_end(k, p):
         await_bytes(side.at[k, p], ring_recv.at[k, p, 2])
@@ -257,31 +276,27 @@
         total = f32(part.at[k, p, t]) + f32(side.at[k, p, 0]) + f32(side.at[k, p, 1])
         for s2 in range(4):
             for s3 in range(4):
-                if p // 2 == 0:
+                if p in (0, 2):
                     rows = (total[s2, 12 * s3 : 12 * s3 + 12], total[s2, 48 + 4 * s3 : 52 + 4 * s3])
                     rows = jnp.concatenate(rows, 0)
-                elif p // 2 == 1:
+                elif p in (4, 5):
                     rows = total[s2, 16 * s3 : 16 * s3 + 16]
                 else:
                     rows = [total[s2, 16 * hb + 4 * s3 : 16 * hb + 4 * s3 + 4] for hb in range(4)]
                     rows = jnp.concatenate(rows, 0)
-                plane_out[k, p, s2, s3] = rows.astype(BF)
-
-        @pl.loop(1, 16)
-        def _(step):
-            plane_copy(k, p, step).start()
+                plane_out[k, p // 2, s2, s3, p % 2] = rows.astype(BF)
 
     def ring_last(k, p):
-        await_bytes(plane_in.at[k, p, pl.ds(1, 15)], plane_recv.at[k, p])
         _, second, third = orders[p]
-        total = f32(plane_out.at[k, p, where[second], where[third]])
+        total = f32(plane_out.at[k, p // 2, where[second], where[third], p % 2])
         for step in range(1, 16):
-            total += f32(plane_in.at[k, p, step])
-        lanes = slice(256 * (p % 2), 256 * (p % 2) + 256)
-        if p // 2 == 0:
+            total += f32(plane_in.at[k, p // 2, step, p % 2])
+        half = p % 2 if p in (4, 5) else p // 2
+        lanes = slice(256 * half, 256 * half + 256)
+        if p in (0, 2):
             oqkv_ref[:, k, lanes] = total[0:12]
             oproj_ref[k, :, lanes] = total[12:16]
-        elif p // 2 == 1:
+        elif p in (4, 5):
             oup_ref[k, :, lanes] = total
         else:
             for hb in range(4):
@@ -294,8 +309,9 @@
 
     def keep(k, p, first, second, rows, g):
         for s in range(2):
-            at = (first, second) if orders[p + s][0] == orders[p][0] else (second, first)
-            part[k, p + s, at[0], at[1], rows, :] = g[:, 256 * s : 256 * s + 256]
+            q = p + s if p == 4 else p + 2 * s
+            at = (first, second) if orders[q][0] == orders[p][0] else (second, first)
+            part[k, q, at[0], at[1], rows, :] = g[:, 256 * s : 256 * s + 256]
 
     def grads_a(k):
         for name in ("n1", "att", "ep", "eq"):
@@ -308,7 +324,7 @@
             for at in range(8):
                 keep(k, 0, 2 * hi + at % 2, at // 2, slice(48, 64), g[16 * at : 16 * at + 16])
         ring_start(k, 0)
-        ring_start(k, 1)
+        ring_start(k, 2)
 
     def grads_b(k):
         for name in ("n2", "eu"):
@@ -317,9 +333,9 @@
             g = both(k, "eu", hi, n2[k], pn2[k]).astype(BF)
             for at in range(32):
                 row = (2 * hi + at // 4 % 2) * 16
-                keep(k, 2, at % 4, at // 8, slice(row, row + 16), g[16 * at : 16 * at + 16])
-        ring_start(k, 2)
-        ring_start(k, 3)
+                keep(k, 4, at % 4, at // 8, slice(row, row + 16), g[16 * at : 16 * at + 16])
+        ring_start(k, 4)
+        ring_start(k, 5)
 
     def grads_c(k):
         for name in ("hs", "ed"):
@@ -330,9 +346,9 @@
                 g = both(k, "ed", hi, hs[k, :, cols], phs[k, :, cols]).astype(BF)
                 for at in range(8):
                     row = 16 * hb
-                    keep(k, 4, 2 * hi + at % 2, at // 2, slice(row, row + 16), g[16 * at : 16 * at + 16])
-        ring_start(k, 4)
-        ring_start(k, 5)
+                    keep(k, 1, 2 * hi + at % 2, at // 2, slice(row, row + 16), g[16 * at : 16 * at + 16])
+        ring_start(k, 1)
+        ring_start(k, 3)
 
     def exchange(event, forward):
         for q in range(4):
@@ -517,32 +533,33 @@
 
     def amid_one(half):
         if half == 1:
-            mids(1, (4, 5))
+            mids(1, (1, 3))
 
     backward(1, got(0), nothing, nothing, amid_one)
     d_second = backward_end(1)
     put(3, d_second.astype(BF))
     exchange(3, False)
     grads_a(1)
-    mids(1, (2, 3))
+    mids(1, (4, 5))
     arrive(3)
 
     def up_zero():
-        ends(1, (4, 5))
-        mids(1, (0, 1))
+        mids(1, (0, 2))
 
     def proj_zero():
-        ends(1, (2, 3))
+        ends(1, (1, 3, 4, 5))
+        plane_start(1, 4, 2)
 
     def amid_zero(half):
         if half == 0:
-            ends(1, (0, 1))
+            ends(1, (0, 2))
+            plane_start(1, 0, 2)
+            plane_start(1, 2, 2)
         else:
-            mids(0, (4, 5, 2, 3))
+            mids(0, (1, 3, 4, 5))
 
     backward(0, got(3), up_zero, proj_zero, amid_zero)
     grads_a(0)
-    ends(0, (4, 5))
     d_first = backward_end(0)
     nat2[...] = tn(ton_ref[...], d_first.astype(BF)).astype(BF)
     for half in range(2):
@@ -561,8 +578,12 @@
                     16 * g : 16 * g + 16, 128 * lane_block : 128 * lane_block + 128
                 ]
     lane_start(1)
-    mids(0, (0, 1))
-    ends(0, (2, 3))
+    mids(0, (0, 2))
+    ends(0, (1, 3))
+    plane_start(0, 1, 1)
+    plane_start(0, 3, 1)
+    ends(0, (4, 5))
+    plane_start(0, 4, 2)
     arrive(2)
     natural = tn(son_ref[...], recv[2].reshape(4 * SLOT, C)).astype(BF)
     mixed_ref[...] = natural.reshape(T // LEV, LEV, C)
@@ -573,9 +594,16 @@
         stores[-1].start()
 
     store(mixed_ref, mixed_hbm)
+    ends(0, (0, 2))
+    plane_start(0, 0, 1)
+    plane_start(0, 2, 1)
+    for group in (0, 2, 4):
+        plane_arrive(1, group, 2)
     lasts(1, range(6))
-    ends(0, (0, 1))
-    lasts(0, (4, 5, 2, 3))
+    plane_arrive(0, 1, 1)
+    plane_arrive(0, 3, 1)
+    plane_arrive(0, 4, 2)
+    lasts(0, (1, 3, 4, 5))
     store(oup_ref, oup_hbm)
     store(odown_ref, odown_hbm)
     lane_finish(1)
@@ -584,7 +612,9 @@
         n = 8 if half == 0 else 4
         denc_ref[8 * half : 8 * half + n] = rows[0 : 16 * n].reshape(n, 16, 32 * WLON)
     store(denc_ref, denc_hbm)
-    lasts(0, (0, 1))
+    plane_arrive(0, 0, 1)
+    plane_arrive(0, 2, 1)
+    lasts(0, (0, 2))
     store(oqkv_ref, oqkv_hbm)
     store(oproj_ref, oproj_hbm)
     for event in range(4):
@@ -594,7 +624,8 @@
             taken(k, name, pair_send)
         for p in range(6):
             await_bytes(part.at[k, p, pl.ds(0, 3)], ring_send.at[k, p])
-            await_bytes(plane_in.at[k, p, pl.ds(1, 15)], plane_send.at[k, p])
+    for k, p, count in planes:
+        await_bytes(plane_bytes(k, p, count), plane_send.at[k, p])
     for copy in stores:
         copy.wait()
 
@@ -643,7 +674,7 @@
             V((2, 2, T, 384), BF), V((2, 2, T, 128), BF), V((2, 2, T, 512), BF), V((2, 2, T, 128), BF),
             dma((2, 8)), dma((2, 8)),
             V((2, 6, 4, 4, 64, 256), BF), V((2, 6, 2, 2, 64, 256), BF), V((2, 6, 2, 2, 64, 256), BF),
-            V((2, 6, 2, 4, 64, 256), BF), V((2, 6, 4, 4, 16, 256), BF), V((2, 6, 16, 16, 256), BF),
+            V((2, 6, 2, 4, 64, 256), BF), V((2, 3, 4, 4, 2, 16, 256), BF), V((2, 3, 16, 2, 16, 256), BF),
             dma((2, 6)), dma((2, 6, 3)), dma((2, 6)), dma((2, 6)),
         ],
         compiler_params=pltpu.CompilerParams(

time: 84.5 us -> 85 us (level); the launches traced: 83.4 us -> 84.9 us
  Pallas kernels: 82.8 us -> 84.2 us
    pallas_call x1, Pallas kernels: 81 us -> 82.4 us  [layers(): pl.pallas_call(layers_kernel, out_shape=shapes, in_specs=[hbm] * 11, out_...]
where the time goes in v7:
time: 85 us; the launch traced here: 84.9 us
  Pallas kernels  84.2 us (99%)
    pallas_call x1, Pallas kernels, layers(): pl.pallas_call(layers_kernel, out_shape=shapes, in_specs=[hbm] * 11, out_...  82.4 us
    pallas_call x1, Pallas kernels, layers(): pl.pallas_call(copies_kernel, out_shape=shapes, in_specs=[vmem] * 6, out_...  1.84 us

profile of v7, /device:TPU:1, one launch (start us, length us, event | category | flops | bytes accessed | tf_op | source)
XLA Modules:
  0.0 84.9 jit_solution(9260784567454707823)
XLA Ops:
  0.6 82.4 %shard_map.154 = (bf16[72,2,512]{2,1,0:T(2,128)(2,1)}, bf16[12,16,384]{2,1,0:T(8,128)(2,1)}, f32[12,2,512]{2,1,0:T(2,128)}, f32[2,4,512]{2,1,0:T(4,128)}, f32[2,16,512]{2,1,0:T(8,128)}, /*index=5*/f32[2,4,2048]{2,1,0:T(4,128)}) custom-call(bf16[12,16,384]{2,1,0:T(8,128)(2,1)} %bitcast.12, bf16[72,2,512]{2,1,0:T(2,128)(2,1)} %bitcast.13, ...), custom_call_target="tpu_custom_call" | custom-call | tf_op jit(solution)/shard_map/pallas_call | solution.py:651
  83.0 1.8 %shard_map.155 = (bf16[72,2,512]{2,1,0:T(2,128)(2,1)}, bf16[12,16,384]{2,1,0:T(8,128)(2,1)}, f32[12,2,512]{2,1,0:T(2,128)}, f32[2,4,512]{2,1,0:T(4,128)}, f32[2,16,512]{2,1,0:T(8,128)}, /*index=5*/f32[2,4,2048]{2,1,0:T(4,128)}) custom-call(bf16[72,2,512]{2,1,0:T(2,128)(2,1)} %get-tuple-element.18.refs_0_, bf16[12,16,384]{2,1,0:T(8,128)(2,1)} %get-tuple-element.19.refs_1_, ...), custom_call_target="tpu_custom_call" | custom-call | tf_op jit(solution)/shard_map/pallas_call | solution.py:684

commit v8 on v7

--- a/solution.py
+++ b/solution.py
@@ -399,10 +399,9 @@
             cols = slice(s * C, s * C + C)
             us[k, :, cols] = nn(n1[k], wqkv[k, :, cols]).astype(BF)
 
-        @pl.loop(0, 4)
-        def _(g):
+        for g in range(4):
             def part(w):
-                return us[k, :, pl.ds(pl.multiple_of(w * C + g * 128, 128), 128)]
+                return us[k, :, pl.ds(w * C + g * 128, 128)]
 
             q, key, v = part(0), part(1), part(2)
             stacked = jnp.concatenate([q * m for m in head_mask], 0)
@@ -415,7 +414,7 @@
             total = jnp.zeros((T, 128), F32)
             for s in range(4):
                 total += jnp.where(inside[s], out[T * s : T * s + T], 0.0)
-            att[k, :, pl.ds(pl.multiple_of(g * 128, 128), 128)] = total.astype(BF)
+            att[k, :, pl.ds(g * 128, 128)] = total.astype(BF)
 
         give(k, "att")
         fetches[4 * k + 1].wait()
@@ -452,20 +451,20 @@
             eu[k, :, cols] = (dh * gp[k, :, cols]).astype(BF)
 
         give(k, "eu")
+        grads_c(k)
         after_up()
         dn2 = nt(eu[k], wup[k]).astype(BF).astype(F32)
         dm = acc[...] + norm_back(dn2, n2h[k], r2[k][:, 0:1])
         acc[...] = dm
         ep[k] = dm.astype(BF)
         give(k, "ep")
-        grads_c(k)
+        grads_b(k)
         dab[...] = nt(ep[k], wproj[k]).astype(BF)
-        grads_b(k)
         after_proj()
 
         def heads(g):
             def at(w):
-                return pl.ds(pl.multiple_of(w * C + g * 128, 128), 128)
+                return slice(w * C + g * 128, w * C + g * 128 + 128)
 
             q, key, v = us[k, :, at(0)], us[k, :, at(1)], us[k, :, at(2)]
             da = dab[:, at(0)]
@@ -491,7 +490,8 @@
             eq[k, :, at(2)] = dv.astype(BF)
 
         for half in range(2):
-            pl.loop(2 * half, 2 * half + 2)(heads)
+            for g in range(2 * half, 2 * half + 2):
+                heads(g)
             amid(half)
         give(k, "eq")
 
@@ -577,8 +577,8 @@
                 leave2[8 * g + lane_block, half] = moved[
                     16 * g : 16 * g + 16, 128 * lane_block : 128 * lane_block + 128
                 ]
+    mids(0, (0, 2))
     lane_start(1)
-    mids(0, (0, 2))
     ends(0, (1, 3))
     plane_start(0, 1, 1)
     plane_start(0, 3, 1)

time: 85 us -> 81.3 us (0.956)
  Pallas kernels: 84.2 us -> 80.5 us
    pallas_call x1, Pallas kernels: 82.4 us -> 78.6 us  [layers(): pl.pallas_call(layers_kernel, out_shape=shapes, in_specs=[hbm] * 11, out_...]
where the time goes in v8:
time: 81.3 us; the launch traced here: 81.1 us
  Pallas kernels  80.5 us (99%)
    pallas_call x1, Pallas kernels, layers(): pl.pallas_call(layers_kernel, out_shape=shapes, in_specs=[hbm] * 11, out_...  78.6 us
    pallas_call x1, Pallas kernels, layers(): pl.pallas_call(copies_kernel, out_shape=shapes, in_specs=[vmem] * 6, out_...  1.84 us

profile of v8, /device:TPU:1, one launch (start us, length us, event | category | flops | bytes accessed | tf_op | source)
XLA Modules:
  0.0 81.1 jit_solution(14018032176590210048)
XLA Ops:
  0.6 78.6 %shard_map.154 = (bf16[72,2,512]{2,1,0:T(2,128)(2,1)}, bf16[12,16,384]{2,1,0:T(8,128)(2,1)}, f32[12,2,512]{2,1,0:T(2,128)}, f32[2,4,512]{2,1,0:T(4,128)}, f32[2,16,512]{2,1,0:T(8,128)}, /*index=5*/f32[2,4,2048]{2,1,0:T(4,128)}) custom-call(bf16[12,16,384]{2,1,0:T(8,128)(2,1)} %bitcast.12, bf16[72,2,512]{2,1,0:T(2,128)(2,1)} %bitcast.13, ...), custom_call_target="tpu_custom_call" | custom-call | tf_op jit(solution)/shard_map/pallas_call | solution.py:651
  79.3 1.8 %shard_map.155 = (bf16[72,2,512]{2,1,0:T(2,128)(2,1)}, bf16[12,16,384]{2,1,0:T(8,128)(2,1)}, f32[12,2,512]{2,1,0:T(2,128)}, f32[2,4,512]{2,1,0:T(4,128)}, f32[2,16,512]{2,1,0:T(8,128)}, /*index=5*/f32[2,4,2048]{2,1,0:T(4,128)}) custom-call(bf16[72,2,512]{2,1,0:T(2,128)(2,1)} %get-tuple-element.18.refs_0_, bf16[12,16,384]{2,1,0:T(8,128)(2,1)} %get-tuple-element.19.refs_1_, ...), custom_call_target="tpu_custom_call" | custom-call | tf_op jit(solution)/shard_map/pallas_call | solution.py:684

commit v9 on v8

--- a/solution.py
+++ b/solution.py
@@ -133,8 +133,7 @@
     for other in greeted:
         pl.semaphore_signal(barrier, inc=1, device_id=other, device_id_type=MESH)
 
-    @pl.loop(1, nlon)
-    def _(step):
+    for step in range(1, nlon):
         pl.semaphore_signal(barrier, inc=1, device_id=device(0, step), device_id_type=MESH)
 
     for name in ("up", "son", "tos", "ton", "swap"):
@@ -163,8 +162,7 @@
         )
 
     def lane_start(event):
-        @pl.loop(1, nlon)
-        def _(step):
+        for step in range(1, nlon):
             lane_copy(step, event).start()
 
         if event == 0:
@@ -247,7 +245,7 @@
 
     def plane_copy(k, p, count, step):
         _, second, third = orders[p]
-        d2, d3 = step // 4, lax.rem(step, 4)
+        d2, d3 = divmod(step, 4)
         held = pl.ds(p % 2, count)
         src = plane_out.at[k, p // 2, lax.rem(where[second] + d2, 4), lax.rem(where[third] + d3, 4), held]
         return pltpu.make_async_remote_copy(
@@ -258,8 +256,7 @@
     def plane_start(k, p, count):
         planes.append((k, p, count))
 
-        @pl.loop(1, 16)
-        def _(step):
+        for step in range(1, 16):
             plane_copy(k, p, count, step).start()
 
     planes = []
@@ -505,7 +502,7 @@
     inputs["swap"].wait()
     lane_finish(0)
     for half in range(2):
-        moved = nn(came[half].reshape(64, 1024), swap[...]).astype(BF)
+        moved = nn(came[half].reshape(64, 1024), swap[:, 0 : 1024 - 512 * half]).astype(BF)
         for lr in range(8 if half == 0 else 4):
             for g in range(4):
                 at = (slice(128 * half + 16 * lr, 128 * half + 16 * lr + 16), slice(128 * g, 128 * g + 128))
@@ -555,23 +552,21 @@
             ends(1, (0, 2))
             plane_start(1, 0, 2)
             plane_start(1, 2, 2)
+            mids(0, (1, 3))
         else:
-            mids(0, (1, 3, 4, 5))
+            mids(0, (4, 5))
 
     backward(0, got(3), up_zero, proj_zero, amid_zero)
     grads_a(0)
     d_first = backward_end(0)
     nat2[...] = tn(ton_ref[...], d_first.astype(BF)).astype(BF)
     for half in range(2):
-        for lr in range(8):
+        for lr in range(8 if half == 0 else 4):
             for g in range(4):
                 at = (slice(16 * g, 16 * g + 16), slice(128 * lr, 128 * lr + 128))
-                if half == 1 and lr >= 4:
-                    turned[half, at[0], at[1]] = jnp.zeros((16, 128), BF)
-                else:
-                    row = 128 * half + 16 * lr
-                    turned[half, at[0], at[1]] = nat2[row : row + 16, 128 * g : 128 * g + 128]
-        moved = nn(turned[half], swap[...]).astype(BF)
+                row = 128 * half + 16 * lr
+                turned[half, at[0], at[1]] = nat2[row : row + 16, 128 * g : 128 * g + 128]
+        moved = nn(turned[half, :, 0 : 1024 - 512 * half], swap[0 : 1024 - 512 * half]).astype(BF)
         for g in range(4):
             for lane_block in range(8):
                 leave2[8 * g + lane_block, half] = moved[

time: 81.3 us -> 79.8 us (0.982)
  Pallas kernels: 80.5 us -> 79.1 us
    pallas_call x1, Pallas kernels: 78.6 us -> 77.2 us  [layers(): pl.pallas_call(layers_kernel, out_shape=shapes, in_specs=[hbm] * 11, out_...]
where the time goes in v9:
time: 79.8 us; the launch traced here: 79.7 us
  Pallas kernels  79.1 us (99%)
    pallas_call x1, Pallas kernels, layers(): pl.pallas_call(layers_kernel, out_shape=shapes, in_specs=[hbm] * 11, out_...  77.2 us
    pallas_call x1, Pallas kernels, layers(): pl.pallas_call(copies_kernel, out_shape=shapes, in_specs=[vmem] * 6, out_...  1.84 us

profile of v9, /device:TPU:1, one launch (start us, length us, event | category | flops | bytes accessed | tf_op | source)
XLA Modules:
  0.0 79.7 jit_solution(17393198981618893113)
XLA Ops:
  0.6 77.2 %shard_map.154 = (bf16[72,2,512]{2,1,0:T(2,128)(2,1)}, bf16[12,16,384]{2,1,0:T(8,128)(2,1)}, f32[12,2,512]{2,1,0:T(2,128)}, f32[2,4,512]{2,1,0:T(4,128)}, f32[2,16,512]{2,1,0:T(8,128)}, /*index=5*/f32[2,4,2048]{2,1,0:T(4,128)}) custom-call(bf16[12,16,384]{2,1,0:T(8,128)(2,1)} %bitcast.12, bf16[72,2,512]{2,1,0:T(2,128)(2,1)} %bitcast.13, ...), custom_call_target="tpu_custom_call" | custom-call | tf_op jit(solution)/shard_map/pallas_call | solution.py:646
  77.9 1.8 %shard_map.155 = (bf16[72,2,512]{2,1,0:T(2,128)(2,1)}, bf16[12,16,384]{2,1,0:T(8,128)(2,1)}, f32[12,2,512]{2,1,0:T(2,128)}, f32[2,4,512]{2,1,0:T(4,128)}, f32[2,16,512]{2,1,0:T(8,128)}, /*index=5*/f32[2,4,2048]{2,1,0:T(4,128)}) custom-call(bf16[72,2,512]{2,1,0:T(2,128)(2,1)} %get-tuple-element.18.refs_0_, bf16[12,16,384]{2,1,0:T(8,128)(2,1)} %get-tuple-element.19.refs_1_, ...), custom_call_target="tpu_custom_call" | custom-call | tf_op jit(solution)/shard_map/pallas_call | solution.py:679

commit v10 on v9

--- a/solution.py
+++ b/solution.py
@@ -311,15 +311,17 @@
             part[k, q, at[0], at[1], rows, :] = g[:, 256 * s : 256 * s + 256]
 
     def grads_a(k):
-        for name in ("n1", "att", "ep", "eq"):
+        for name in ("att", "ep", "n1"):
             take(k, name)
+        for hi in range(2):
+            g = both(k, "ep", hi, att[k], patt[k]).astype(BF)
+            for at in range(8):
+                keep(k, 0, 2 * hi + at % 2, at // 2, slice(48, 64), g[16 * at : 16 * at + 16])
+        take(k, "eq")
         for hi in range(2):
             g = both(k, "eq", hi, n1[k], pn1[k]).astype(BF)
             for at in range(8):
                 keep(k, 0, 2 * hi + at % 2, at // 2, slice(0, 48), g[48 * at : 48 * at + 48])
-            g = both(k, "ep", hi, att[k], patt[k]).astype(BF)
-            for at in range(8):
-                keep(k, 0, 2 * hi + at % 2, at // 2, slice(48, 64), g[16 * at : 16 * at + 16])
         ring_start(k, 0)
         ring_start(k, 2)
 
@@ -489,8 +491,9 @@
         for half in range(2):
             for g in range(2 * half, 2 * half + 2):
                 heads(g)
+            if half == 1:
+                give(k, "eq")
             amid(half)
-        give(k, "eq")
 
     def backward_end(k):
         dn1 = nt(eq[k], wqkv[k]).astype(BF).astype(F32)
@@ -557,9 +560,9 @@
             mids(0, (4, 5))
 
     backward(0, got(3), up_zero, proj_zero, amid_zero)
+    d_first = backward_end(0).astype(BF)
     grads_a(0)
-    d_first = backward_end(0)
-    nat2[...] = tn(ton_ref[...], d_first.astype(BF)).astype(BF)
+    nat2[...] = tn(ton_ref[...], d_first).astype(BF)
     for half in range(2):
         for lr in range(8 if half == 0 else 4):
             for g in range(4):

time: 79.8 us -> 79.4 us (level)
  Pallas kernels: 79.1 us -> 77.9 us
    pallas_call x1, Pallas kernels: 77.2 us -> 76.1 us  [layers(): pl.pallas_call(layers_kernel, out_shape=shapes, in_specs=[hbm] * 11, out_...]
where the time goes in v10:
time: 79.4 us; the launch traced here: 78.6 us
  Pallas kernels  77.9 us (98%)
    pallas_call x1, Pallas kernels, layers(): pl.pallas_call(layers_kernel, out_shape=shapes, in_specs=[hbm] * 11, out_...  76.1 us
    pallas_call x1, Pallas kernels, layers(): pl.pallas_call(copies_kernel, out_shape=shapes, in_specs=[vmem] * 6, out_...  1.84 us

profile of v10, /device:TPU:1, one launch (start us, length us, event | category | flops | bytes accessed | tf_op | source)
XLA Modules:
  0.0 78.6 jit_solution(3392025094327887375)
XLA Ops:
  0.6 76.1 %shard_map.154 = (bf16[72,2,512]{2,1,0:T(2,128)(2,1)}, bf16[12,16,384]{2,1,0:T(8,128)(2,1)}, f32[12,2,512]{2,1,0:T(2,128)}, f32[2,4,512]{2,1,0:T(4,128)}, f32[2,16,512]{2,1,0:T(8,128)}, /*index=5*/f32[2,4,2048]{2,1,0:T(4,128)}) custom-call(bf16[12,16,384]{2,1,0:T(8,128)(2,1)} %bitcast.12, bf16[72,2,512]{2,1,0:T(2,128)(2,1)} %bitcast.13, ...), custom_call_target="tpu_custom_call" | custom-call | tf_op jit(solution)/shard_map/pallas_call | solution.py:649
  76.7 1.8 %shard_map.155 = (bf16[72,2,512]{2,1,0:T(2,128)(2,1)}, bf16[12,16,384]{2,1,0:T(8,128)(2,1)}, f32[12,2,512]{2,1,0:T(2,128)}, f32[2,4,512]{2,1,0:T(4,128)}, f32[2,16,512]{2,1,0:T(8,128)}, /*index=5*/f32[2,4,2048]{2,1,0:T(4,128)}) custom-call(bf16[72,2,512]{2,1,0:T(2,128)(2,1)} %get-tuple-element.18.refs_0_, bf16[12,16,384]{2,1,0:T(8,128)(2,1)} %get-tuple-element.19.refs_1_, ...), custom_call_target="tpu_custom_call" | custom-call | tf_op jit(solution)/shard_map/pallas_call | solution.py:682
